TPU v7x, 128 devices: a whole 4x4x4 slice. The times are simulated.
128 devices in a mesh: row: 32 (over y, z, x_lo), col: 4 (over x_hi, core).
Axes of the slice: x: 4 (x_hi: 2, x_lo: 2; x = x_hi * 2 + x_lo), y: 4, z: 4, core: 2. Of those that a mesh axis runs over, the one named last changes fastest.
Arguments:
- pair: bfloat16 [1536, 1536, 128], P('row', 'col'), may hold values from -6 to 6
- w_in: bfloat16 [128, 512], replicated, may hold values from -0.5 to 0.5
- w_gate: bfloat16 [128, 128], replicated, may hold values from -0.5 to 0.5
- w_out: bfloat16 [128, 128], replicated, may hold values from -0.5 to 0.5
Outputs:
- swapped: bfloat16 [1536, 1536, 128], P('row', 'col')
All inputs are finite; a program needn't handle non-finite values.
Results may differ from a plain program's by a relative error of at most 0.0053.
Values may be sent and summed in bfloat16 or wider, within the bound.
No kernel may reach another device: no remote copies, remote signals or barrier semaphores. Data moves between devices by JAX's collectives and lax.ppermute only.
A program may use at most 192 MiB of HBM per device.

v0:
```python
import jax
import jax.numpy as jnp
from jax import lax
from jax.sharding import PartitionSpec as P


def as_sent(array):
    return jax.tree.map(lambda a: a.astype(jnp.bfloat16) if a.dtype == jnp.float32 else a, array)


def normalize(values):
    mean = jnp.mean(values, axis=-1, keepdims=True)
    centred = values - mean
    spread = jnp.mean(centred * centred, axis=-1, keepdims=True)
    return centred * lax.rsqrt(spread + 1e-05)


def combine(z_rows, normed, x_rows, w_gate, w_out):
    width = z_rows.shape[-1]
    hidden = x_rows.shape[-1]
    gate = jax.nn.sigmoid(
        jnp.dot(normed.reshape(-1, width), w_gate, preferred_element_type=jnp.float32)
    )
    x_normed = normalize(x_rows.astype(jnp.float32)).astype(jnp.bfloat16)
    update = jnp.dot(x_normed.reshape(-1, hidden), w_out, preferred_element_type=jnp.float32)
    merged = z_rows.astype(jnp.float32).reshape(-1, width) + gate * update
    return merged.reshape(z_rows.shape).astype(jnp.bfloat16)


def to_channels(planes):
    moved = jax.tree.map(
        lambda part, own: part.astype(own.dtype),
        lax.all_to_all(
            lax.all_to_all(as_sent(planes), "row", split_axis=0, concat_axis=1, tiled=True),
            "col",
            split_axis=0,
            concat_axis=2,
            tiled=True,
        ),
        planes,
    )
    return tuple(moved)


def from_channels(planes):
    row_count = lax.axis_size("row")
    col_count = lax.axis_size("col")
    count, total, _ = planes[0].shape
    rows = total // row_count
    cols = total // col_count
    lifted = tuple((piece[None] for piece in planes))
    moved = jax.tree.map(
        lambda part, own: part.astype(own.dtype),
        lax.all_to_all(
            lax.all_to_all(as_sent(lifted), "row", split_axis=2, concat_axis=0, tiled=True),
            "col",
            split_axis=3,
            concat_axis=1,
            tiled=True,
        ),
        lifted,
    )
    return tuple((piece.reshape(-1, rows, cols) for piece in moved))


def multiply(left_planes, right_planes):
    crossed = jnp.einsum(
        "hik,hjk->hij", left_planes, right_planes, preferred_element_type=jnp.float32
    )
    return crossed.astype(jnp.bfloat16)


def on_device(pair, w_in, w_gate, w_out):
    rows, cols, width = pair.shape
    hidden = w_out.shape[0]
    normed = normalize(pair.astype(jnp.float32)).astype(jnp.bfloat16)
    proj = jnp.dot(normed.reshape(-1, width), w_in, preferred_element_type=jnp.float32)
    left = (jax.nn.sigmoid(proj[:, :hidden]) * proj[:, hidden : 2 * hidden]).astype(jnp.bfloat16)
    right = (jax.nn.sigmoid(proj[:, 2 * hidden : 3 * hidden]) * proj[:, 3 * hidden :]).astype(
        jnp.bfloat16
    )
    left_planes = jnp.transpose(left.reshape(rows, cols, hidden), (2, 0, 1))
    right_planes = jnp.transpose(right.reshape(rows, cols, hidden), (2, 0, 1))
    owned = to_channels((left_planes, right_planes))
    crossed = multiply(owned[0], owned[1])
    returned = from_channels((crossed,))[0]
    updated = combine(pair, normed, jnp.transpose(returned, (1, 2, 0)), w_gate, w_out)
    planes = to_channels((jnp.transpose(updated, (2, 0, 1)),))[0]
    turned = from_channels((jnp.transpose(planes, (0, 2, 1)),))[0]
    return jnp.transpose(turned, (1, 2, 0))


def solution(mesh):
    placed = (P("row", "col", None), P(), P(), P())
    return jax.shard_map(
        on_device, mesh=mesh, in_specs=placed, out_specs=P("row", "col", None), check_vma=False
    )
```

profile of v0, /device:TPU:1, one launch (start us, length us, event | category | flops | bytes accessed | tf_op | source)
XLA Modules:
  0.0 1102.3 jit_solution(6476597944099946470)
XLA Ops:
  0.0 0.0 copy-start
  0.0 3.8 convert_reduce_fusion
  3.8 5.5 multiply_reduce_fusion.1
  9.3 5.9 multiply_convert_fusion.1
  15.3 0.0 copy-start.3
  15.3 14.7 %fusion.16 = f32[18432,512]{1,0:T(8,128)} fusion(bf16[18432,128]{1,0:T(8,128)(2,1)S(1)} %bitcast.104, bf16[128,512]{1,0:T(8,128)(2,1)S(1)} %copy-done), kind=kOutput, calls=%fused_computation.36 | convolution fusion | flops 2415919104 | bytes 42598400 | tf_op jit(solution)/shard_map/dot_general | solution.py:77
  30.0 0.0 copy-done.3
  30.0 17.8 %fusion.9 = (bf16[18432,128]{1,0:T(8,128)(2,1)}, bf16[18432,128]{1,0:T(8,128)(2,1)}) fusion(f32[18432,512]{1,0:T(8,128)} %fusion.16), kind=kLoop, calls=%fused_computation.14 | loop fusion | flops 23592960 | bytes 47185920 | tf_op jit(solution)/shard_map/convert_element_type | solution.py:78
  47.8 7.1 copy.58
  54.9 9.9 all-to-all-start
  64.8 7.2 copy.60
  72.0 67.2 %all-to-all-done = bf16[128,48,384]{2,1,0:T(8,128)(2,1)} async-done(((bf16[128,48,384]{2,1,0:T(8,128)(2,1)}), bf16[128,48,384]{2,1,0:T(8,128)(2,1)}, u32[]{:S(2)}, u32[]{:S(2)}) %all-to-all-start) | async-done | bytes 4718624 | tf_op jit(solution)/shard_map/all_to_all | solution.py:34
  139.2 4.9 all-to-all-start.2
  144.1 4.9 copy.59
  149.1 66.8 %all-to-all-done.2 = bf16[128,48,384]{2,1,0:T(8,128)(2,1)} async-done(((bf16[128,48,384]{2,1,0:T(8,128)(2,1)}), bf16[128,48,384]{2,1,0:T(8,128)(2,1)}, u32[]{:S(2)}, u32[]{:S(2)}) %all-to-all-start.2) | async-done | bytes 4718624 | tf_op jit(solution)/shard_map/all_to_all | solution.py:34
  215.8 6.8 all-to-all-start.1
  222.7 5.1 copy.61
  227.7 49.5 %all-to-all-done.1 = bf16[4,1536,384]{2,1,0:T(8,128)(2,1)} async-done(((bf16[4,1536,384]{2,1,0:T(8,128)(2,1)}), bf16[4,1536,384]{2,1,0:T(8,128)(2,1)}, u32[]{:S(2)}, u32[]{:S(2)}) %all-to-all-start.1) | async-done | bytes 4718624 | tf_op jit(solution)/shard_map/all_to_all | solution.py:33
  277.2 59.1 %all_to_all.150 = bf16[4,1536,384]{2,1,0:T(8,128)(2,1)S(1)} all-to-all(bf16[4,1536,384]{2,1,0:T(8,128)(2,1)} %bitcast.112), channel_id=1, replica_groups=mesh['row'=32,'col'=4] {'col'}, dimensions={0} | all-to-all | bytes 9437184 | tf_op jit(solution)/shard_map/all_to_all | solution.py:33
  336.3 9.4 fusion.13
  345.8 52.2 %copy.81 = bf16[1,1,1536,1536]{3,1,0,2:T(2,128)(2,1)} copy(bf16[1,1,1536,1536]{3,2,1,0:T(8,128)(2,1)S(1)} %fusion.13) | data formatting | bytes 9437184 | tf_op jit(solution)/shard_map/broadcast_in_dim | solution.py:51
  398.0 0.6 broadcast.55
  398.6 32.0 %reduce = bf16[1536,1536]{1,0:T(8,128)(2,1)} reduce(bf16[1536,1,1,1536]{3,2,1,0:T(2,128)(2,1)} %bitcast.99, bf16[]{:T(256)} %broadcast.55), dimensions={1,2}, to_apply=%bitcast.89.reduce_sub_computation | reduce | bytes 9437186
  430.6 8.2 reshape.82
  438.8 61.4 %all_to_all.151 = bf16[32,2,36864]{2,1,0:T(2,128)(2,1)} all-to-all(bf16[32,2,36864]{2,1,0:T(2,128)(2,1)} %reshape.82), channel_id=1, replica_groups=mesh['row'=32,'col'=4] {'row'}, dimensions={0} | all-to-all | bytes 9437184 | tf_op jit(solution)/shard_map/all_to_all | solution.py:55
  500.2 20.2 %reshape.83 = bf16[1536,1,1,1536]{3,2,1,0:T(2,128)(2,1)} reshape(bf16[32,2,36864]{2,1,0:T(2,128)(2,1)} %all_to_all.151) | data formatting | bytes 9437184
  520.5 7.1 copy.75
  527.5 17.8 %copy.63 = bf16[32,1,48,1536]{2,0,1,3:T(8,128)(2,1)} copy(bf16[32,1,48,1536]{3,2,0,1:T(8,128)(2,1)} %bitcast.113) | data formatting | bytes 9437184 | tf_op jit(solution)/shard_map/all_to_all | solution.py:55
  545.3 21.5 %reshape.84 = bf16[4,2,294912]{2,1,0:T(2,128)(2,1)} reshape(bf16[1536,1,32,48]{3,2,1,0:T(8,128)(2,1)} %bitcast.93) | data formatting | bytes 9437184
  566.8 7.5 all-to-all-start.5
  574.3 8.5 fusion.4
  582.8 45.9 %all-to-all-done.5 = bf16[4,2,294912]{2,1,0:T(2,128)(2,1)} async-done(((bf16[4,2,294912]{2,1,0:T(2,128)(2,1)}), bf16[4,2,294912]{2,1,0:T(2,128)(2,1)}, u32[]{:S(2)}, u32[]{:S(2)}) %all-to-all-start.5) | async-done | bytes 4718624 | tf_op jit(solution)/shard_map/all_to_all | solution.py:54
  628.8 14.9 %reshape.85 = bf16[1536,1,32,48]{3,2,1,0:T(8,128)(2,1)} reshape(bf16[4,2,294912]{2,1,0:T(2,128)(2,1)} %all-to-all-done.5) | data formatting | bytes 9437184
  643.6 13.7 %copy.64 = bf16[32,1,48,1536]{3,2,1,0:T(8,128)(2,1)} copy(bf16[32,1,48,1536]{2,0,1,3:T(8,128)(2,1)} %bitcast.94) | data formatting | bytes 9437184 | tf_op jit(solution)/shard_map/all_to_all | solution.py:54
  657.3 9.9 reshape.80
  667.2 4.7 copy.65
  671.9 1.1 bitcast_reduce_fusion
  673.0 1.6 multiply_reduce_fusion
  674.6 1.5 multiply_convert_fusion
  676.2 0.0 slice-start
  676.2 0.0 slice-start.1
  676.2 0.0 copy-start.4
  676.2 1.2 copy.77
  677.4 0.9 slice-done
  678.4 0.1 slice-done.1
  678.5 6.5 fusion.3
  684.9 7.0 copy.66
  692.0 60.4 %all_to_all.152 = bf16[128,48,384]{2,1,0:T(8,128)(2,1)S(1)} all-to-all(bf16[128,48,384]{2,1,0:T(8,128)(2,1)} %bitcast.114), channel_id=1, replica_groups=mesh['row'=32,'col'=4] {'row'}, dimensions={0} | all-to-all | bytes 9437184 | tf_op jit(solution)/shard_map/all_to_all | solution.py:34
  752.4 0.5 copy.67
  752.9 59.8 %all_to_all.153 = bf16[4,1536,384]{2,1,0:T(8,128)(2,1)} all-to-all(bf16[4,1536,384]{2,1,0:T(8,128)(2,1)S(1)} %bitcast.116), channel_id=1, replica_groups=mesh['row'=32,'col'=4] {'col'}, dimensions={0} | all-to-all | bytes 9437184 | tf_op jit(solution)/shard_map/all_to_all | solution.py:33
  812.7 6.6 copy.68
  819.3 9.6 copy.80
  828.9 32.0 %reduce.1 = bf16[1536,1536]{1,0:T(8,128)(2,1)} reduce(bf16[1536,1,1,1536]{3,2,1,0:T(2,128)(2,1)} %bitcast.100, bf16[]{:T(256)} %broadcast.55), dimensions={1,2}, to_apply=%bitcast.88.reduce_sub_computation | reduce | bytes 9437186
  860.9 8.2 reshape.86
  869.0 61.3 %all_to_all.154 = bf16[32,2,36864]{2,1,0:T(2,128)(2,1)} all-to-all(bf16[32,2,36864]{2,1,0:T(2,128)(2,1)} %reshape.86), channel_id=1, replica_groups=mesh['row'=32,'col'=4] {'row'}, dimensions={0} | all-to-all | bytes 9437184 | tf_op jit(solution)/shard_map/all_to_all | solution.py:55
  930.3 20.2 %reshape.87 = bf16[1536,1,1,1536]{3,2,1,0:T(2,128)(2,1)} reshape(bf16[32,2,36864]{2,1,0:T(2,128)(2,1)} %all_to_all.154) | data formatting | bytes 9437184
  950.5 7.2 copy.76
  957.7 17.8 %copy.70 = bf16[32,1,48,1536]{2,0,1,3:T(8,128)(2,1)} copy(bf16[32,1,48,1536]{3,2,0,1:T(8,128)(2,1)} %bitcast.118) | data formatting | bytes 9437184 | tf_op jit(solution)/shard_map/all_to_all | solution.py:55
  975.5 21.5 %reshape.88 = bf16[4,2,294912]{2,1,0:T(2,128)(2,1)} reshape(bf16[1536,1,32,48]{3,2,1,0:T(8,128)(2,1)} %bitcast.95) | data formatting | bytes 9437184
  997.0 62.8 %all_to_all.155 = bf16[4,2,294912]{2,1,0:T(2,128)(2,1)} all-to-all(bf16[4,2,294912]{2,1,0:T(2,128)(2,1)} %reshape.88), channel_id=1, replica_groups=mesh['row'=32,'col'=4] {'col'}, dimensions={0} | all-to-all | bytes 9437184 | tf_op jit(solution)/shard_map/all_to_all | solution.py:54
  1059.8 14.9 %reshape.89 = bf16[1536,1,32,48]{3,2,1,0:T(8,128)(2,1)} reshape(bf16[4,2,294912]{2,1,0:T(2,128)(2,1)} %all_to_all.155) | data formatting | bytes 9437184
  1074.6 14.8 %copy.74 = bf16[32,1,48,4,384]{4,3,2,0,1:T(4,128)(2,1)} copy(bf16[32,1,48,4,384]{2,0,4,3,1:T(8,128)(2,1)} %bitcast.96) | data formatting | bytes 9437184 | tf_op jit(solution)/shard_map/all_to_all | solution.py:54
  1089.4 5.3 copy.72
  1094.8 7.0 copy.73
  (13 shorter events, 0.1 us)
Async XLA Ops:
  0.0 15.3 %copy-start = (bf16[128,512]{1,0:T(8,128)(2,1)S(1)}, bf16[128,512]{1,0:T(8,128)(2,1)}, u32[]{:S(2)}) copy-start(bf16[128,512]{1,0:T(8,128)(2,1)} %param.5) | copy-start | bytes 393220
  0.0 3.8 copy-start.2
  15.3 14.7 %copy-start.3 = (bf16[48,384,128]{2,1,0:T(8,128)(2,1)}, bf16[48,384,128]{2,1,0:T(8,128)(2,1)S(1)}, u32[]{:S(2)}) copy-start(bf16[48,384,128]{2,1,0:T(8,128)(2,1)S(1)} %multiply_convert_fusion.1) | copy-start | bytes 14155780
  54.9 84.4 %all-to-all-start = ((bf16[128,48,384]{2,1,0:T(8,128)(2,1)}), bf16[128,48,384]{2,1,0:T(8,128)(2,1)}, u32[]{:S(2)}, u32[]{:S(2)}) async-start(bf16[128,48,384]{2,1,0:T(8,128)(2,1)} %bitcast.111), calls=%async_computation | async-start | bytes 9437184 | tf_op jit(solution)/shard_map/all_to_all | solution.py:34
  139.2 76.6 %all-to-all-start.2 = ((bf16[128,48,384]{2,1,0:T(8,128)(2,1)}), bf16[128,48,384]{2,1,0:T(8,128)(2,1)}, u32[]{:S(2)}, u32[]{:S(2)}) async-start(bf16[128,48,384]{2,1,0:T(8,128)(2,1)} %bitcast.109), calls=%async_computation.2 | async-start | bytes 9437184 | tf_op jit(solution)/shard_map/all_to_all | solution.py:34
  215.8 61.4 %all-to-all-start.1 = ((bf16[4,1536,384]{2,1,0:T(8,128)(2,1)}), bf16[4,1536,384]{2,1,0:T(8,128)(2,1)}, u32[]{:S(2)}, u32[]{:S(2)}) async-start(bf16[4,1536,384]{2,1,0:T(8,128)(2,1)} %bitcast.110), calls=%async_computation.1 | async-start | bytes 9437184 | tf_op jit(solution)/shard_map/all_to_all | solution.py:33
  566.8 7.5 copy-start.5
  566.8 62.0 %all-to-all-start.5 = ((bf16[4,2,294912]{2,1,0:T(2,128)(2,1)}), bf16[4,2,294912]{2,1,0:T(2,128)(2,1)}, u32[]{:S(2)}, u32[]{:S(2)}) async-start(bf16[4,2,294912]{2,1,0:T(2,128)(2,1)} %reshape.84), calls=%async_computation.5 | async-start | bytes 9437184 | tf_op jit(solution)/shard_map/all_to_all | solution.py:54
  676.2 2.2 slice-start
  676.2 2.3 slice-start.1
  676.2 2.3 copy-start.4
  1094.8 7.0 copy-start.1
where the time goes:
time: 1110 us; the launch traced here: 1100 us
  blocking collectives  365 us (33%)
  local copies, waits for them, and re-layouts  338 us (30%)
  waiting for transfers between devices  229 us (21%)
  other arithmetic  101 us (9%)
  matrix products  39.1 us (4%)
  starting transfers between devices  29.1 us (3%)
    unnamed x28, local copies, waits for them, and re-layouts  147 us
    all_to_all x2, waiting for transfers between devices, to_channels(): lax.all_to_all(as_sent(planes), 'row', split_axis=0, concat_axis=1, tiled...  134 us
    all_to_all x2, blocking collectives, from_channels(): lax.all_to_all(as_sent(lifted), 'row', split_axis=2, concat_axis=0, tiled...  123 us
    all_to_all x2, blocking collectives, to_channels(): lax.all_to_all(lax.all_to_all(as_sent(planes), 'row', split_axis=0, conca...  119 us
    unnamed x3, other arithmetic  64 us
    all_to_all x1, blocking collectives, from_channels(): lax.all_to_all(lax.all_to_all(as_sent(lifted), 'row', split_axis=2, conca...  62.8 us
    broadcast_in_dim x2, local copies, waits for them, and re-layouts, from_channels(): lifted = tuple((piece[None] for piece in planes))  61.9 us
    all_to_all x1, blocking collectives, to_channels(): lax.all_to_all(as_sent(planes), 'row', split_axis=0, concat_axis=1, tiled...  60.4 us
  transfers between devices with their start and end apart: 4, of which 4 were waited for; matrix products, arithmetic and copies ran while one was open for 2% of the time, Pallas kernels for 0%

commit v1 on v0

v1 whole, which is shorter than its diff:
```python
import jax
import jax.numpy as jnp
from jax import lax
from jax.experimental import pallas as pl
from jax.experimental.pallas import tpu as pltpu
from jax.sharding import PartitionSpec as P

ALL = ("row", "col")
VMEM_LIMIT = 56 * 1024 * 1024


def sigmoid(x):
    return 0.5 * jnp.tanh(0.5 * x) + 0.5


def params():
    return pltpu.CompilerParams(vmem_limit_bytes=VMEM_LIMIT)


def project_kernel(x_ref, wt_ref, a_ref, b_ref, sa, sb):
    groups = x_ref.shape[0]
    hidden = a_ref.shape[0]

    for g in range(0, groups, 2):
        parts = []
        for q in range(2):
            v = x_ref[g + q].T.astype(jnp.float32)
            mean = jnp.mean(v, axis=0, keepdims=True)
            v = v - mean
            var = jnp.mean(v * v, axis=0, keepdims=True)
            parts.append((v * lax.rsqrt(var + 1e-5)).astype(jnp.bfloat16))
        n = jnp.concatenate(parts, axis=1)
        for dst, k in ((sa, 0), (sb, 2)):
            gate = jnp.dot(wt_ref[pl.ds(k * hidden, hidden), :], n, preferred_element_type=jnp.float32)
            value = jnp.dot(
                wt_ref[pl.ds((k + 1) * hidden, hidden), :], n, preferred_element_type=jnp.float32
            )
            res = sigmoid(gate) * value
            for q in range(2):
                dst[pl.ds(g + q, hidden, stride=groups), :] = res[:, q * 128 : (q + 1) * 128]
    a_ref[...] = sa[...].astype(jnp.bfloat16).reshape(a_ref.shape)
    b_ref[...] = sb[...].astype(jnp.bfloat16).reshape(b_ref.shape)


def project(pair, w_in):
    rows, cols, width = pair.shape
    hidden = w_in.shape[1] // 4
    kg = cols // 128
    gb = 16
    out = jax.ShapeDtypeStruct((hidden, kg, rows, 128), jnp.bfloat16)
    spec = pl.BlockSpec((hidden, None, gb, 128), lambda k, i: (0, k, i, 0))
    return pl.pallas_call(
        project_kernel,
        grid=(kg, rows // gb),
        in_specs=[
            pl.BlockSpec((gb, 128, width), lambda k, i: (i, k, 0)),
            pl.BlockSpec((4 * hidden, width), lambda k, i: (0, 0)),
        ],
        out_specs=[spec, spec],
        out_shape=[out, out],
        scratch_shapes=[pltpu.VMEM((hidden * gb, 128), jnp.float32)] * 2,
        compiler_params=params(),
        cost_estimate=pl.CostEstimate(
            flops=2 * rows * cols * width * hidden * 4,
            bytes_accessed=6 * rows * cols * width,
            transcendentals=2 * rows * cols * hidden,
        ),
        name="project",
    )(pair, w_in.T)


def cross_kernel(b_ref, a_ref, o_ref):
    nb, kgs, rows, _ = b_ref.shape
    na = a_ref.shape[0]
    b = jnp.concatenate(
        [b_ref[:, q].reshape(nb * rows, 128) for q in range(kgs)], axis=1
    )
    step = o_ref.shape[2] * 128 // rows
    for c in range(na // step):
        a = jnp.concatenate(
            [a_ref[pl.ds(c * step, step), q].reshape(step * rows, 128) for q in range(kgs)], axis=1
        )
        res = lax.dot_general(b, a, (((1,), (1,)), ((), ())), preferred_element_type=jnp.float32)
        res = res.astype(jnp.bfloat16)
        for t in range(o_ref.shape[2]):
            o_ref[:, c, t] = res[:, t * 128 : (t + 1) * 128].reshape(nb, rows, 128)


def cross(b_recv, a_recv, row_count, col_count):
    _, kg, rows, _ = b_recv.shape
    b = b_recv.reshape(row_count, col_count * kg, rows, 128)
    a = a_recv.reshape(row_count, col_count * kg, rows, 128)
    kgs = col_count * kg
    nb = 8
    tokens = row_count * rows
    return pl.pallas_call(
        cross_kernel,
        grid=(row_count // nb,),
        in_specs=[
            pl.BlockSpec((nb, kgs, rows, 128), lambda j: (j, 0, 0, 0)),
            pl.BlockSpec((row_count, kgs, rows, 128), lambda j: (0, 0, 0, 0)),
        ],
        out_specs=pl.BlockSpec((nb, col_count, kg, rows, 128), lambda j: (j, 0, 0, 0, 0)),
        out_shape=jax.ShapeDtypeStruct((row_count, col_count, kg, rows, 128), jnp.bfloat16),
        compiler_params=params(),
        cost_estimate=pl.CostEstimate(
            flops=2 * tokens**3, bytes_accessed=6 * tokens * tokens, transcendentals=0
        ),
        name="cross",
    )(b, a)


def gate_kernel(z_ref, w_ref, g_ref):
    jb, cols, width = z_ref.shape
    z = z_ref[...].reshape(jb * cols, width).astype(jnp.float32)
    mean = jnp.mean(z, axis=-1, keepdims=True)
    z = z - mean
    var = jnp.mean(z * z, axis=-1, keepdims=True)
    n = (z * lax.rsqrt(var + 1e-5)).astype(jnp.bfloat16)
    g_ref[...] = sigmoid(
        jnp.dot(n, w_ref[...], preferred_element_type=jnp.float32)
    ).reshape(g_ref.shape)


def gate_of(z, w_gate):
    rows, cols, width = z.shape
    jb = 4
    return pl.pallas_call(
        gate_kernel,
        grid=(rows // jb,),
        in_specs=[
            pl.BlockSpec((jb, cols, width), lambda j: (j, 0, 0)),
            pl.BlockSpec((width, width), lambda j: (0, 0)),
        ],
        out_specs=pl.BlockSpec((jb, cols, width), lambda j: (j, 0, 0)),
        out_shape=jax.ShapeDtypeStruct((rows, cols, width), jnp.float32),
        compiler_params=params(),
        cost_estimate=pl.CostEstimate(
            flops=2 * rows * cols * width * width,
            bytes_accessed=6 * rows * cols * width,
            transcendentals=rows * cols * width,
        ),
        name="gate",
    )(z, w_gate)


def finish_kernel(r_ref, z_ref, g_ref, w_ref, o_ref, s0, s1, s2):
    hidden, groups, jb, _ = r_ref.shape
    scr = (s0, s1, s2)
    for t in range(groups):
        scr[t][...] = r_ref[:, t].astype(jnp.float32).reshape(hidden * jb, 128)
    for j in range(jb):
        for t in range(groups):
            v = scr[t][pl.ds(j, hidden, stride=jb), :]
            mean = jnp.mean(v, axis=0, keepdims=True)
            v = v - mean
            var = jnp.mean(v * v, axis=0, keepdims=True)
            n = (v * lax.rsqrt(var + 1e-5)).astype(jnp.bfloat16)
            update = lax.dot_general(
                n, w_ref[...], (((0,), (0,)), ((), ())), preferred_element_type=jnp.float32
            )
            at = pl.ds(t * 128, 128)
            res = z_ref[j, at].astype(jnp.float32) + g_ref[j, at] * update
            o_ref[j, at] = res.astype(jnp.bfloat16)


def finish(returned, z, gate, w_out):
    hidden, groups, rows, _ = returned.shape
    _, cols, width = z.shape
    jb = 16
    tok = pl.BlockSpec((jb, cols, width), lambda j: (j, 0, 0))
    return pl.pallas_call(
        finish_kernel,
        grid=(rows // jb,),
        in_specs=[
            pl.BlockSpec((hidden, groups, jb, 128), lambda j: (0, 0, j, 0)),
            tok,
            tok,
            pl.BlockSpec((hidden, width), lambda j: (0, 0)),
        ],
        out_specs=tok,
        out_shape=jax.ShapeDtypeStruct((rows, cols, width), jnp.bfloat16),
        scratch_shapes=[pltpu.VMEM((hidden * jb, 128), jnp.float32)] * 3,
        compiler_params=params(),
        cost_estimate=pl.CostEstimate(
            flops=2 * rows * cols * width * hidden,
            bytes_accessed=10 * rows * cols * width,
            transcendentals=0,
        ),
        name="finish",
    )(returned, z, gate, w_out)


def swap_tokens(pair, row_count, col_count):
    rows, cols, width = pair.shape
    low = row_count // col_count
    me = lax.rem(lax.axis_index("row"), low)
    pieces = pair.reshape(rows, low, rows, width)
    got = jnp.zeros((low, rows, rows, width), pair.dtype)
    for s in range(low):
        perm = [
            ((h * low + q) * col_count + c, (c * low + (q ^ s)) * col_count + h)
            for h in range(col_count)
            for q in range(low)
            for c in range(col_count)
        ]
        other = lax.bitwise_xor(me, s)
        piece = lax.dynamic_index_in_dim(pieces, other, 1, keepdims=False)
        moved = lax.ppermute(piece, ALL, perm)
        got = lax.dynamic_update_index_in_dim(got, moved, other, 0)
    return jnp.transpose(got, (2, 0, 1, 3)).reshape(rows, cols, width)


def exchange(x):
    return lax.all_to_all(x, ALL, split_axis=0, concat_axis=0, tiled=True)


def on_device(pair, w_in, w_gate, w_out):
    row_count = lax.axis_size("row")
    col_count = lax.axis_size("col")
    turned = swap_tokens(pair, row_count, col_count)
    a, b = project(pair, w_in)
    a_own = exchange(a)
    b_own = exchange(b)
    crossed = cross(b_own, a_own, row_count, col_count)
    crossed = crossed.reshape((row_count * col_count,) + crossed.shape[2:])
    returned = exchange(crossed)
    return finish(returned, turned, gate_of(turned, w_gate), w_out)


def solution(mesh):
    placed = (P("row", "col", None), P(), P(), P())
    return jax.shard_map(
        on_device, mesh=mesh, in_specs=placed, out_specs=P("row", "col", None), check_vma=False
    )
```

time: 1110 us -> 362 us (0.33)
  local copies, waits for them, and re-layouts: 338 us -> 9.95 us
  blocking collectives: 365 us -> 133 us
  waiting for transfers between devices: 229 us -> 83.1 us
  other arithmetic: 101 us -> 0 us
  Pallas kernels: 0 us -> 54.2 us
  starting transfers between devices: 29.1 us -> 76.2 us
  matrix products: 39.1 us -> 0 us
    all_to_all x6 -> x2, blocking collectives: 365 us -> 133 us  [exchange(): return lax.all_to_all(x, ALL, split_axis=0, concat_axis=0, tiled=True)]
    all_to_all x4 -> x1, waiting for transfers between devices: 229 us -> 0.01 us  [exchange(): return lax.all_to_all(x, ALL, split_axis=0, concat_axis=0, tiled=True)]
    unnamed x28 -> x5, local copies, waits for them, and re-layouts: 147 us -> 3.77 us
    all_to_all x9 -> x0, local copies, waits for them, and re-layouts: 86.5 us -> none  [the longest x2 35.6 us: from_channels(): lax.all_to_all(as_sent(lifted), 'row', split_axis=2, concat_axis=0, tiled...]
    ppermute x0 -> x8, waiting for transfers between devices: none -> 83.1 us  [swap_tokens(): moved = lax.ppermute(piece, ALL, perm)]
    ppermute x0 -> x8, starting transfers between devices: none -> 70.9 us  [swap_tokens(): moved = lax.ppermute(piece, ALL, perm)]
    unnamed x3 -> x0, other arithmetic: 64 us -> none
    broadcast_in_dim x2 -> x1, local copies, waits for them, and re-layouts: 61.9 us -> 1.1 us  [swap_tokens(): got = jnp.zeros((low, rows, rows, width), pair.dtype)]
  transfers between devices with their start and end apart: 4 -> 9, of which waited for: 4 -> 3; matrix products, arithmetic and copies ran while one was open for 2% -> 2% of each run, Pallas kernels for 0% -> 4%
where the time goes in v1:
time: 362 us; the launch traced here: 357 us
  blocking collectives  133 us (37%)
  waiting for transfers between devices  83.1 us (23%)
  starting transfers between devices  76.2 us (21%)
  Pallas kernels  54.2 us (15%)
  local copies, waits for them, and re-layouts  9.95 us (3%)
    all_to_all x2, blocking collectives, exchange(): return lax.all_to_all(x, ALL, split_axis=0, concat_axis=0, tiled=True)  133 us
    ppermute x8, waiting for transfers between devices, swap_tokens(): moved = lax.ppermute(piece, ALL, perm)  83.1 us
    ppermute x8, starting transfers between devices, swap_tokens(): moved = lax.ppermute(piece, ALL, perm)  70.9 us
    pallas_call x1, Pallas kernels, project(): pl.pallas_call(project_kernel, grid=(kg, rows // gb), in_specs=[pl.BlockS...  14.3 us
    pallas_call x1, Pallas kernels, cross(): pl.pallas_call(cross_kernel, grid=(row_count // nb,), in_specs=[pl.BlockS...  14.2 us
    pallas_call x1, Pallas kernels, gate_of(): pl.pallas_call(gate_kernel, grid=(rows // jb,), in_specs=[pl.BlockSpec((j...  13.2 us
    pallas_call x1, Pallas kernels, finish(): pl.pallas_call(finish_kernel, grid=(rows // jb,), in_specs=[pl.BlockSpec(...  12.6 us
  transfers between devices with their start and end apart: 9, of which 3 were waited for; matrix products, arithmetic and copies ran while one was open for 2% of the time, Pallas kernels for 4%

profile of v1, /device:TPU:1, one launch (start us, length us, event | category | flops | bytes accessed | tf_op | source)
XLA Modules:
  0.0 356.7 jit_solution(17163703450302842934)
XLA Ops:
  0.0 1.7 copy.5
  1.7 14.3 %project.1 = (bf16[128,3,48,128]{3,2,1,0:T(8,128)(2,1)}, bf16[128,3,48,128]{3,2,1,0:T(8,128)(2,1)}) custom-call(bf16[48,384,128]{2,1,0:T(8,128)(2,1)} %x_ref.1, bf16[512,128]{1,0:T(8,128)(2,1)} %bitcast.62), custom_call_target="tpu_custom_call" | custom-call | flops 2415919104 | bytes 14155776 | tf_op jit(solution)/shard_map/project/pallas_call | solution.py:52
  16.0 0.0 copy-start.1
  16.0 70.1 %all_to_all.15 = bf16[128,3,48,128]{3,2,1,0:T(8,128)(2,1)} all-to-all(bf16[128,3,48,128]{3,2,1,0:T(8,128)(2,1)} %get-tuple-element.7), channel_id=1, replica_groups=mesh['row'=32,'col'=4] {'row','col'}, dimensions={0} | all-to-all | bytes 9437184 | tf_op jit(solution)/shard_map/all_to_all | solution.py:215
  86.1 0.0 copy-done.1
  86.1 62.9 %all_to_all.16 = bf16[128,3,48,128]{3,2,1,0:T(8,128)(2,1)} all-to-all(bf16[128,3,48,128]{3,2,1,0:T(8,128)(2,1)S(1)} %copy-done.1), channel_id=1, replica_groups=mesh['row'=32,'col'=4] {'row','col'}, dimensions={0} | all-to-all | bytes 9437184 | tf_op jit(solution)/shard_map/all_to_all | solution.py:215
  149.0 14.2 %cross.1 = bf16[32,4,3,48,128]{4,3,2,1,0:T(8,128)(2,1)} custom-call(bf16[32,12,48,128]{3,2,1,0:T(8,128)(2,1)} %bitcast.52, bf16[32,12,48,128]{3,2,1,0:T(8,128)(2,1)} %bitcast.53), custom_call_target="tpu_custom_call" | custom-call | flops 7247757312 | bytes 14155776 | tf_op jit(solution)/shard_map/cross/pallas_call | solution.py:96
  163.2 5.3 %all-to-all-start.2 = ((bf16[128,3,48,128]{3,2,1,0:T(8,128)(2,1)}), bf16[128,3,48,128]{3,2,1,0:T(8,128)(2,1)}, u32[]{:S(2)}, u32[]{:S(2)}) async-start(bf16[128,3,48,128]{3,2,1,0:T(8,128)(2,1)} %bitcast.51), calls=%async_computation.2 | async-start | bytes 9437184 | tf_op jit(solution)/shard_map/all_to_all | solution.py:215
  168.6 3.2 constant_dynamic-slice_fusion
  171.8 0.2 copy.29
  171.9 3.6 %collective-permute-start = (bf16[48,48,128]{2,0,1:T(8,128)(2,1)S(1)}, bf16[48,48,128]{2,0,1:T(8,128)(2,1)S(1)}, u32[]{:S(2)}, u32[]{:S(2)}) collective-permute-start(bf16[48,48,128]{2,0,1:T(8,128)(2,1)S(1)} %bitcast.61), channel_id=1, source_target_pairs={{0,0},{1,32},{2,64},{3,96},{4,4},{5,36},{6,68},{7,100},{8,8},{9,40... | collective-permute-start | bytes 1769480 | tf_op jit(solution)/shard_map/ppermute | solution.py:209
  175.5 0.2 copy.28
  175.7 1.2 collective-permute-start.1
  176.9 0.2 copy.27
  177.1 2.7 collective-permute-start.2
  179.8 0.2 copy.26
  180.0 0.1 collective-permute-start.3
  180.1 0.2 copy.25
  180.3 4.5 %collective-permute-start.4 = (bf16[48,48,128]{2,0,1:T(8,128)(2,1)S(1)}, bf16[48,48,128]{2,0,1:T(8,128)(2,1)S(1)}, u32[]{:S(2)}, u32[]{:S(2)}) collective-permute-start(bf16[48,48,128]{2,0,1:T(8,128)(2,1)S(1)} %bitcast.56), channel_id=1, source_target_pairs={{0,16},{1,48},{2,80},{3,112},{4,20},{5,52},{6,84},{7,116},{8,24},{... | collective-permute-start | bytes 1769480 | tf_op jit(solution)/shard_map/ppermute | solution.py:209
  184.7 0.2 copy.22
  184.9 0.2 copy.23
  185.0 0.2 copy.24
  185.2 72.2 %collective-permute-done = bf16[48,48,128]{2,0,1:T(8,128)(2,1)S(1)} collective-permute-done((bf16[48,48,128]{2,0,1:T(8,128)(2,1)S(1)}, bf16[48,48,128]{2,0,1:T(8,128)(2,1)S(1)}, u32[]{:S(2)}, u32[]{:S(2)}) %collective-permute-start) | collective-permute-done | bytes 589856 | tf_op jit(solution)/shard_map/ppermute | solution.py:209
  257.4 8.4 %collective-permute-start.5 = (bf16[48,48,128]{2,0,1:T(8,128)(2,1)S(1)}, bf16[48,48,128]{2,0,1:T(8,128)(2,1)S(1)}, u32[]{:S(2)}, u32[]{:S(2)}) collective-permute-start(bf16[48,48,128]{2,0,1:T(8,128)(2,1)S(1)} %bitcast.58), channel_id=1, source_target_pairs={{0,20},{1,52},{2,84},{3,116},{4,16},{5,48},{6,80},{7,112},{8,28},{... | collective-permute-start | bytes 1769480 | tf_op jit(solution)/shard_map/ppermute | solution.py:209
  265.8 1.1 broadcast_in_dim.28
  266.9 0.1 bitcast_dynamic-update-slice_fusion.7
  267.0 0.0 collective-permute-done.1
  267.0 12.8 %collective-permute-start.6 = (bf16[48,48,128]{2,0,1:T(8,128)(2,1)S(1)}, bf16[48,48,128]{2,0,1:T(8,128)(2,1)S(1)}, u32[]{:S(2)}, u32[]{:S(2)}) collective-permute-start(bf16[48,48,128]{2,0,1:T(8,128)(2,1)S(1)} %bitcast.55), channel_id=1, source_target_pairs={{0,24},{1,56},{2,88},{3,120},{4,28},{5,60},{6,92},{7,124},{8,16},{... | collective-permute-start | bytes 1769480 | tf_op jit(solution)/shard_map/ppermute | solution.py:209
  279.8 0.1 bitcast_dynamic-update-slice_fusion.6
  279.9 0.0 collective-permute-done.2
  279.9 37.6 %collective-permute-start.7 = (bf16[48,48,128]{2,0,1:T(8,128)(2,1)S(1)}, bf16[48,48,128]{2,0,1:T(8,128)(2,1)S(1)}, u32[]{:S(2)}, u32[]{:S(2)}) collective-permute-start(bf16[48,48,128]{2,0,1:T(8,128)(2,1)S(1)} %bitcast.54), channel_id=1, source_target_pairs={{0,28},{1,60},{2,92},{3,124},{4,24},{5,56},{6,88},{7,120},{8,20},{... | collective-permute-start | bytes 1769480 | tf_op jit(solution)/shard_map/ppermute | solution.py:209
  317.5 0.1 bitcast_dynamic-update-slice_fusion.5
  317.6 0.0 collective-permute-done.3
  317.6 0.1 bitcast_dynamic-update-slice_fusion.4
  317.7 0.0 collective-permute-done.4
  317.7 0.1 bitcast_dynamic-update-slice_fusion.3
  317.8 0.0 collective-permute-done.5
  317.8 0.1 bitcast_dynamic-update-slice_fusion.2
  317.9 1.2 collective-permute-done.6
  319.0 0.1 bitcast_dynamic-update-slice_fusion.1
  319.1 9.7 %collective-permute-done.7 = bf16[48,48,128]{2,0,1:T(8,128)(2,1)S(1)} collective-permute-done((bf16[48,48,128]{2,0,1:T(8,128)(2,1)S(1)}, bf16[48,48,128]{2,0,1:T(8,128)(2,1)S(1)}, u32[]{:S(2)}, u32[]{:S(2)}) %collective-permute-start.7) | collective-permute-done | bytes 589856 | tf_op jit(solution)/shard_map/ppermute | solution.py:209
  328.8 0.1 bitcast_dynamic-update-slice_fusion
  328.9 0.0 copy-start
  328.9 2.1 copy-done
  331.0 13.2 %gate.1.g_ref = f32[48,384,128]{2,1,0:T(8,128)} custom-call(bf16[48,384,128]{2,1,0:T(8,128)(2,1)} %bitcast.48, bf16[128,128]{1,0:T(8,128)(2,1)} %w_ref.2), custom_call_target="tpu_custom_call" | custom-call | flops 603979776 | bytes 14155776 | tf_op jit(solution)/shard_map/gate/pallas_call | solution.py:128
  344.2 0.0 all-to-all-done.2.r_ref
  344.2 12.6 %finish.1 = bf16[48,384,128]{2,1,0:T(8,128)(2,1)} custom-call(bf16[128,3,48,128]{3,2,1,0:T(8,128)(2,1)} %all-to-all-done.2.r_ref, bf16[48,384,128]{2,1,0:T(8,128)(2,1)} %bitcast.49, f32[48,384,128]{2,1,0:T(8,128)} %gate.1.g_ref, bf16[128,128]{1,0:T(8,128)(2,1)} %w_ref.3), custom_call_target="tpu_custom_call" | custom-call | flops 603979776 | bytes 23592960 | tf_op jit(solution)/shard_map/finish/pallas_call | solution.py:172
Async XLA Ops:
  16.0 70.1 %copy-start.1 = (bf16[128,3,48,128]{3,2,1,0:T(8,128)(2,1)S(1)}, bf16[128,3,48,128]{3,2,1,0:T(8,128)(2,1)}, u32[]{:S(2)}) copy-start(bf16[128,3,48,128]{3,2,1,0:T(8,128)(2,1)} %get-tuple-element.8) | copy-start | bytes 14155780
  163.2 181.0 %all-to-all-start.2 = ((bf16[128,3,48,128]{3,2,1,0:T(8,128)(2,1)}), bf16[128,3,48,128]{3,2,1,0:T(8,128)(2,1)}, u32[]{:S(2)}, u32[]{:S(2)}) async-start(bf16[128,3,48,128]{3,2,1,0:T(8,128)(2,1)} %bitcast.51), calls=%async_computation.2 | async-start | bytes 9437184 | tf_op jit(solution)/shard_map/all_to_all | solution.py:215
  171.9 85.5 %collective-permute-start = (bf16[48,48,128]{2,0,1:T(8,128)(2,1)S(1)}, bf16[48,48,128]{2,0,1:T(8,128)(2,1)S(1)}, u32[]{:S(2)}, u32[]{:S(2)}) collective-permute-start(bf16[48,48,128]{2,0,1:T(8,128)(2,1)S(1)} %bitcast.61), channel_id=1, source_target_pairs={{0,0},{1,32},{2,64},{3,96},{4,4},{5,36},{6,68},{7,100},{8,8},{9,40... | collective-permute-start | bytes 1769480 | tf_op jit(solution)/shard_map/ppermute | solution.py:209
  175.7 91.3 %collective-permute-start.1 = (bf16[48,48,128]{2,0,1:T(8,128)(2,1)S(1)}, bf16[48,48,128]{2,0,1:T(8,128)(2,1)S(1)}, u32[]{:S(2)}, u32[]{:S(2)}) collective-permute-start(bf16[48,48,128]{2,0,1:T(8,128)(2,1)S(1)} %bitcast.60), channel_id=1, source_target_pairs={{0,4},{1,36},{2,68},{3,100},{4,0},{5,32},{6,64},{7,96},{8,12},{9,4... | collective-permute-start | bytes 1769480 | tf_op jit(solution)/shard_map/ppermute | solution.py:209
  177.1 102.8 %collective-permute-start.2 = (bf16[48,48,128]{2,0,1:T(8,128)(2,1)S(1)}, bf16[48,48,128]{2,0,1:T(8,128)(2,1)S(1)}, u32[]{:S(2)}, u32[]{:S(2)}) collective-permute-start(bf16[48,48,128]{2,0,1:T(8,128)(2,1)S(1)} %bitcast.59), channel_id=1, source_target_pairs={{0,8},{1,40},{2,72},{3,104},{4,12},{5,44},{6,76},{7,108},{8,0},{9,... | collective-permute-start | bytes 1769480 | tf_op jit(solution)/shard_map/ppermute | solution.py:209
  180.0 137.6 %collective-permute-start.3 = (bf16[48,48,128]{2,0,1:T(8,128)(2,1)S(1)}, bf16[48,48,128]{2,0,1:T(8,128)(2,1)S(1)}, u32[]{:S(2)}, u32[]{:S(2)}) collective-permute-start(bf16[48,48,128]{2,0,1:T(8,128)(2,1)S(1)} %bitcast.57), channel_id=1, source_target_pairs={{0,12},{1,44},{2,76},{3,108},{4,8},{5,40},{6,72},{7,104},{8,4},{9,... | collective-permute-start | bytes 1769480 | tf_op jit(solution)/shard_map/ppermute | solution.py:209
  180.3 137.4 %collective-permute-start.4 = (bf16[48,48,128]{2,0,1:T(8,128)(2,1)S(1)}, bf16[48,48,128]{2,0,1:T(8,128)(2,1)S(1)}, u32[]{:S(2)}, u32[]{:S(2)}) collective-permute-start(bf16[48,48,128]{2,0,1:T(8,128)(2,1)S(1)} %bitcast.56), channel_id=1, source_target_pairs={{0,16},{1,48},{2,80},{3,112},{4,20},{5,52},{6,84},{7,116},{8,24},{... | collective-permute-start | bytes 1769480 | tf_op jit(solution)/shard_map/ppermute | solution.py:209
  257.4 60.4 %collective-permute-start.5 = (bf16[48,48,128]{2,0,1:T(8,128)(2,1)S(1)}, bf16[48,48,128]{2,0,1:T(8,128)(2,1)S(1)}, u32[]{:S(2)}, u32[]{:S(2)}) collective-permute-start(bf16[48,48,128]{2,0,1:T(8,128)(2,1)S(1)} %bitcast.58), channel_id=1, source_target_pairs={{0,20},{1,52},{2,84},{3,116},{4,16},{5,48},{6,80},{7,112},{8,28},{... | collective-permute-start | bytes 1769480 | tf_op jit(solution)/shard_map/ppermute | solution.py:209
  267.0 52.0 %collective-permute-start.6 = (bf16[48,48,128]{2,0,1:T(8,128)(2,1)S(1)}, bf16[48,48,128]{2,0,1:T(8,128)(2,1)S(1)}, u32[]{:S(2)}, u32[]{:S(2)}) collective-permute-start(bf16[48,48,128]{2,0,1:T(8,128)(2,1)S(1)} %bitcast.55), channel_id=1, source_target_pairs={{0,24},{1,56},{2,88},{3,120},{4,28},{5,60},{6,92},{7,124},{8,16},{... | collective-permute-start | bytes 1769480 | tf_op jit(solution)/shard_map/ppermute | solution.py:209
  279.9 48.9 %collective-permute-start.7 = (bf16[48,48,128]{2,0,1:T(8,128)(2,1)S(1)}, bf16[48,48,128]{2,0,1:T(8,128)(2,1)S(1)}, u32[]{:S(2)}, u32[]{:S(2)}) collective-permute-start(bf16[48,48,128]{2,0,1:T(8,128)(2,1)S(1)} %bitcast.54), channel_id=1, source_target_pairs={{0,28},{1,60},{2,92},{3,124},{4,24},{5,56},{6,88},{7,120},{8,20},{... | collective-permute-start | bytes 1769480 | tf_op jit(solution)/shard_map/ppermute | solution.py:209
  328.9 2.1 copy-start

commit v2 on v1

v2 whole, which is shorter than its diff:
```python
import jax
import jax.numpy as jnp
from jax import lax
from jax.experimental import pallas as pl
from jax.experimental.pallas import tpu as pltpu
from jax.sharding import PartitionSpec as P

ALL = ("row", "col")
GB = 16
EARLY = 7
VMEM_LIMIT = 56 * 1024 * 1024


def sigmoid(x):
    return 0.5 * jnp.tanh(0.5 * x) + 0.5


def params():
    return pltpu.CompilerParams(vmem_limit_bytes=VMEM_LIMIT)


def project_kernel(x_ref, wt_ref, o_ref, sa, sb):
    groups = x_ref.shape[0]
    hidden = o_ref.shape[0]

    for g in range(0, groups, 2):
        parts = []
        for q in range(2):
            v = x_ref[g + q].T.astype(jnp.float32)
            mean = jnp.mean(v, axis=0, keepdims=True)
            v = v - mean
            var = jnp.mean(v * v, axis=0, keepdims=True)
            parts.append((v * lax.rsqrt(var + 1e-5)).astype(jnp.bfloat16))
        n = jnp.concatenate(parts, axis=1)
        for dst, k in ((sa, 0), (sb, 2)):
            gate = jnp.dot(wt_ref[pl.ds(k * hidden, hidden), :], n, preferred_element_type=jnp.float32)
            value = jnp.dot(
                wt_ref[pl.ds((k + 1) * hidden, hidden), :], n, preferred_element_type=jnp.float32
            )
            res = sigmoid(gate) * value
            for q in range(2):
                dst[pl.ds(g + q, hidden, stride=groups), :] = res[:, q * 128 : (q + 1) * 128]
    for p, src in ((0, sa), (1, sb)):
        o_ref[:, p] = src[...].astype(jnp.bfloat16).reshape(hidden, groups, 128)


def project(pair, w_in):
    rows, cols, width = pair.shape
    hidden = w_in.shape[1] // 4
    kg = cols // 128
    return pl.pallas_call(
        project_kernel,
        grid=(kg, rows // GB),
        in_specs=[
            pl.BlockSpec((GB, 128, width), lambda k, i: (i, k, 0)),
            pl.BlockSpec((4 * hidden, width), lambda k, i: (0, 0)),
        ],
        out_specs=pl.BlockSpec((hidden, None, None, 2, GB, 128), lambda k, i: (0, k, i, 0, 0, 0)),
        out_shape=jax.ShapeDtypeStruct((hidden, kg, rows // GB, 2, GB, 128), jnp.bfloat16),
        scratch_shapes=[pltpu.VMEM((hidden * GB, 128), jnp.float32)] * 2,
        compiler_params=params(),
        cost_estimate=pl.CostEstimate(
            flops=2 * rows * cols * width * hidden * 4,
            bytes_accessed=6 * rows * cols * width,
            transcendentals=2 * rows * cols * hidden,
        ),
        name="project",
    )(pair, w_in.T)


def plane_rows(ref, first, count):
    _, kgs, parts, group, lanes = ref.shape
    return jnp.concatenate(
        [ref[pl.ds(first, count), q].reshape(count * parts * group, lanes) for q in range(kgs)],
        axis=1,
    )


def cross_kernel(b_ref, a_ref, o_ref):
    nb, col_count, kg, rows, _ = o_ref.shape
    b = plane_rows(b_ref, 0, nb)
    step = kg * 128 // rows
    for c in range(col_count):
        a = plane_rows(a_ref, c * step, step)
        res = lax.dot_general(b, a, (((1,), (1,)), ((), ())), preferred_element_type=jnp.float32)
        res = res.astype(jnp.bfloat16)
        for t in range(kg):
            o_ref[:, c, t] = res[:, t * 128 : (t + 1) * 128].reshape(nb, rows, 128)


def cross(own, row_count, col_count):
    _, kg, parts, _, group, _ = own.shape
    rows = parts * group
    kgs = col_count * kg
    own = own.reshape(row_count, kgs, parts, 2, group, 128)
    nb = 8
    tokens = row_count * rows
    return pl.pallas_call(
        cross_kernel,
        grid=(row_count // nb,),
        in_specs=[
            pl.BlockSpec((nb, kgs, parts, None, group, 128), lambda j: (j, 0, 0, 1, 0, 0)),
            pl.BlockSpec((row_count, kgs, parts, None, group, 128), lambda j: (0, 0, 0, 0, 0, 0)),
        ],
        out_specs=pl.BlockSpec((nb, col_count, kg, rows, 128), lambda j: (j, 0, 0, 0, 0)),
        out_shape=jax.ShapeDtypeStruct((row_count, col_count, kg, rows, 128), jnp.bfloat16),
        compiler_params=params(),
        cost_estimate=pl.CostEstimate(
            flops=2 * tokens**3, bytes_accessed=6 * tokens * tokens, transcendentals=0
        ),
        name="cross",
    )(own, own).reshape(row_count * col_count, kg, rows, 128)


def gate_kernel(z_ref, w_ref, g_ref):
    jb, cols, width = z_ref.shape
    z = z_ref[...].reshape(jb * cols, width).astype(jnp.float32)
    mean = jnp.mean(z, axis=-1, keepdims=True)
    z = z - mean
    var = jnp.mean(z * z, axis=-1, keepdims=True)
    n = (z * lax.rsqrt(var + 1e-5)).astype(jnp.bfloat16)
    g_ref[...] = sigmoid(
        jnp.dot(n, w_ref[...], preferred_element_type=jnp.float32)
    ).reshape(g_ref.shape)


def gate_of(z, w_gate):
    rows, cols, width = z.shape
    jb = 4
    return pl.pallas_call(
        gate_kernel,
        grid=(rows // jb,),
        in_specs=[
            pl.BlockSpec((jb, cols, width), lambda j: (j, 0, 0)),
            pl.BlockSpec((width, width), lambda j: (0, 0)),
        ],
        out_specs=pl.BlockSpec((jb, cols, width), lambda j: (j, 0, 0)),
        out_shape=jax.ShapeDtypeStruct((rows, cols, width), jnp.float32),
        compiler_params=params(),
        cost_estimate=pl.CostEstimate(
            flops=2 * rows * cols * width * width,
            bytes_accessed=6 * rows * cols * width,
            transcendentals=rows * cols * width,
        ),
        name="gate",
    )(z, w_gate)


def finish_kernel(r_ref, z_ref, g_ref, w_ref, o_ref, scr):
    hidden, jb, _ = r_ref.shape
    scr[...] = r_ref[...].astype(jnp.float32).reshape(hidden * jb, 128)
    for j in range(jb):
        v = scr[pl.ds(j, hidden, stride=jb), :]
        mean = jnp.mean(v, axis=0, keepdims=True)
        v = v - mean
        var = jnp.mean(v * v, axis=0, keepdims=True)
        n = (v * lax.rsqrt(var + 1e-5)).astype(jnp.bfloat16)
        update = lax.dot_general(
            n, w_ref[...], (((0,), (0,)), ((), ())), preferred_element_type=jnp.float32
        )
        o_ref[j] = (z_ref[j].astype(jnp.float32) + g_ref[j] * update).astype(jnp.bfloat16)


def finish(returned, z, gate, w_out):
    hidden, groups, rows, _ = returned.shape
    _, cols, width = z.shape
    tok = pl.BlockSpec((GB, 128, width), lambda j, t: (j, t, 0))
    return pl.pallas_call(
        finish_kernel,
        grid=(rows // GB, groups),
        in_specs=[
            pl.BlockSpec((hidden, None, GB, 128), lambda j, t: (0, t, j, 0)),
            tok,
            tok,
            pl.BlockSpec((hidden, width), lambda j, t: (0, 0)),
        ],
        out_specs=tok,
        out_shape=jax.ShapeDtypeStruct((rows, cols, width), jnp.bfloat16),
        scratch_shapes=[pltpu.VMEM((hidden * GB, 128), jnp.float32)],
        compiler_params=params(),
        cost_estimate=pl.CostEstimate(
            flops=2 * rows * cols * width * hidden,
            bytes_accessed=10 * rows * cols * width,
            transcendentals=0,
        ),
        name="finish",
    )(returned, z, gate, w_out)


def cut(pair, low):
    rows, cols, width = pair.shape
    me = lax.rem(lax.axis_index("row"), low)
    pieces = pair.reshape(rows, low, rows, width)
    return [
        lax.dynamic_index_in_dim(pieces, lax.bitwise_xor(me, s), 1, keepdims=False)
        for s in range(low)
    ]


def send(piece, s, low, high):
    perm = [
        ((h * low + q) * high + c, (c * low + (q ^ s)) * high + h)
        for h in range(high)
        for q in range(low)
        for c in range(high)
    ]
    return lax.ppermute(piece, ALL, perm)


def place(moved):
    low = len(moved)
    rows, _, width = moved[0].shape
    me = lax.rem(lax.axis_index("row"), low)
    got = jnp.zeros((low, rows, rows, width), moved[0].dtype)
    for s, piece in enumerate(moved):
        got = lax.dynamic_update_index_in_dim(got, piece, lax.bitwise_xor(me, s), 0)
    return jnp.transpose(got, (2, 0, 1, 3)).reshape(rows, low * rows, width)


def exchange(x):
    return lax.all_to_all(x, ALL, split_axis=0, concat_axis=0, tiled=True)


def on_device(pair, w_in, w_gate, w_out):
    row_count = lax.axis_size("row")
    col_count = lax.axis_size("col")
    low = row_count // col_count
    pieces = cut(pair, low)
    early = [send(pieces[s], s, low, col_count) for s in range(EARLY)]
    early, both = lax.optimization_barrier((early, project(pair, w_in)))
    own = exchange(both)
    own, rest = lax.optimization_barrier((own, pieces[EARLY:]))
    late = [send(p, EARLY + s, low, col_count) for s, p in enumerate(rest)]
    late, crossed = lax.optimization_barrier((late, cross(own, row_count, col_count)))
    returned = exchange(crossed)
    turned = place(early + late)
    return finish(returned, turned, gate_of(turned, w_gate), w_out)


def solution(mesh):
    placed = (P("row", "col", None), P(), P(), P())
    return jax.shard_map(
        on_device, mesh=mesh, in_specs=placed, out_specs=P("row", "col", None), check_vma=False
    )
```

time: 362 us -> 330 us (0.912); the launches traced: 357 us -> 328 us
  blocking collectives: 133 us -> 0 us
  waiting for transfers between devices: 83.1 us -> 204 us
  starting transfers between devices: 76.2 us -> 51.5 us
  local copies, waits for them, and re-layouts: 9.95 us -> 17 us
    all_to_all x1 -> x2, waiting for transfers between devices: 0.01 us -> 150 us  [exchange(): return lax.all_to_all(x, ALL, split_axis=0, concat_axis=0, tiled=True)]
    all_to_all x2 -> x0, blocking collectives: 133 us -> none  [exchange(): return lax.all_to_all(x, ALL, split_axis=0, concat_axis=0, tiled=True)]
    ppermute x8, starting transfers between devices: 70.9 us -> 27.1 us  [send(): return lax.ppermute(piece, ALL, perm)]
    ppermute x8, waiting for transfers between devices: 83.1 us -> 53.9 us  [send(): return lax.ppermute(piece, ALL, perm)]
    all_to_all x1 -> x2, starting transfers between devices: 5.29 us -> 24.4 us  [exchange(): return lax.all_to_all(x, ALL, split_axis=0, concat_axis=0, tiled=True)]
    dynamic_slice x9, local copies, waits for them, and re-layouts: 4.44 us -> 9.3 us  [cut(): lax.dynamic_index_in_dim(pieces, lax.bitwise_xor(me, s), 1, keepdims=False)]
  transfers between devices with their start and end apart: 9 -> 10, of which waited for: 3 -> 6; matrix products, arithmetic and copies ran while one was open for 2% -> 4% of each run, Pallas kernels for 4% -> 13%
where the time goes in v2:
time: 330 us; the launch traced here: 328 us
  waiting for transfers between devices  204 us (62%)
  Pallas kernels  55.5 us (17%)
  starting transfers between devices  51.5 us (16%)
  local copies, waits for them, and re-layouts  17 us (5%)
    all_to_all x2, waiting for transfers between devices, exchange(): return lax.all_to_all(x, ALL, split_axis=0, concat_axis=0, tiled=True)  150 us
    ppermute x8, waiting for transfers between devices, send(): return lax.ppermute(piece, ALL, perm)  53.9 us
    ppermute x8, starting transfers between devices, send(): return lax.ppermute(piece, ALL, perm)  27.1 us
    all_to_all x2, starting transfers between devices, exchange(): return lax.all_to_all(x, ALL, split_axis=0, concat_axis=0, tiled=True)  24.4 us
    pallas_call x1, Pallas kernels, project(): pl.pallas_call(project_kernel, grid=(kg, rows // GB), in_specs=[pl.BlockS...  14.4 us
    pallas_call x1, Pallas kernels, cross(): pl.pallas_call(cross_kernel, grid=(row_count // nb,), in_specs=[pl.BlockS...  14.2 us
    pallas_call x1, Pallas kernels, finish(): pl.pallas_call(finish_kernel, grid=(rows // GB, groups), in_specs=[pl.Blo...  13.7 us
    pallas_call x1, Pallas kernels, gate_of(): pl.pallas_call(gate_kernel, grid=(rows // jb,), in_specs=[pl.BlockSpec((j...  13.2 us
  transfers between devices with their start and end apart: 10, of which 6 were waited for; matrix products, arithmetic and copies ran while one was open for 4% of the time, Pallas kernels for 13%

profile of v2, /device:TPU:1, one launch (start us, length us, event | category | flops | bytes accessed | tf_op | source)
XLA Modules:
  0.0 328.4 jit_solution(3136642449960934147)
XLA Ops:
  0.0 3.1 constant_dynamic-slice_fusion
  3.2 0.2 copy.29
  3.3 4.6 %collective-permute-start = (bf16[48,48,128]{2,0,1:T(8,128)(2,1)S(1)}, bf16[48,48,128]{2,0,1:T(8,128)(2,1)S(1)}, u32[]{:S(2)}, u32[]{:S(2)}) collective-permute-start(bf16[48,48,128]{2,0,1:T(8,128)(2,1)S(1)} %bitcast.52), channel_id=1, source_target_pairs={{0,0},{1,32},{2,64},{3,96},{4,4},{5,36},{6,68},{7,100},{8,8},{9,40... | collective-permute-start | bytes 1769480 | tf_op jit(solution)/shard_map/ppermute | solution.py:207
  7.9 0.2 copy.28
  8.1 1.0 collective-permute-start.1
  9.1 1.0 copy.27
  10.1 3.1 collective-permute-start.2
  13.2 1.0 copy.26
  14.1 0.0 collective-permute-start.3
  14.1 1.0 copy.25
  15.1 4.6 %collective-permute-start.4 = (bf16[48,48,128]{2,0,1:T(8,128)(2,1)}, bf16[48,48,128]{2,0,1:T(8,128)(2,1)S(1)}, u32[]{:S(2)}, u32[]{:S(2)}) collective-permute-start(bf16[48,48,128]{2,0,1:T(8,128)(2,1)} %bitcast.42), channel_id=1, source_target_pairs={{0,16},{1,48},{2,80},{3,112},{4,20},{5,52},{6,84},{7,116},{8,24},{... | collective-permute-start | bytes 1769480 | tf_op jit(solution)/shard_map/ppermute | solution.py:207
  19.7 1.0 copy.24
  20.7 1.0 copy.23
  21.6 22.2 %collective-permute-done = bf16[48,48,128]{2,0,1:T(8,128)(2,1)S(1)} collective-permute-done((bf16[48,48,128]{2,0,1:T(8,128)(2,1)S(1)}, bf16[48,48,128]{2,0,1:T(8,128)(2,1)S(1)}, u32[]{:S(2)}, u32[]{:S(2)}) %collective-permute-start) | collective-permute-done | bytes 589856 | tf_op jit(solution)/shard_map/ppermute | solution.py:207
  43.9 4.5 %collective-permute-start.5 = (bf16[48,48,128]{2,0,1:T(8,128)(2,1)}, bf16[48,48,128]{2,0,1:T(8,128)(2,1)}, u32[]{:S(2)}, u32[]{:S(2)}) collective-permute-start(bf16[48,48,128]{2,0,1:T(8,128)(2,1)} %bitcast.41), channel_id=1, source_target_pairs={{0,20},{1,52},{2,84},{3,116},{4,16},{5,48},{6,80},{7,112},{8,28},{... | collective-permute-start | bytes 1769480 | tf_op jit(solution)/shard_map/ppermute | solution.py:207
  48.4 0.0 collective-permute-done.1
  48.4 1.6 collective-permute-start.6
  50.0 1.7 copy.12
  51.7 14.4 %project.1 = bf16[128,3,3,2,16,128]{5,4,3,2,1,0:T(8,128)(2,1)} custom-call(bf16[48,384,128]{2,1,0:T(8,128)(2,1)} %x_ref.1, bf16[512,128]{1,0:T(8,128)(2,1)} %bitcast.54), custom_call_target="tpu_custom_call" | custom-call | flops 2415919104 | bytes 14155776 | tf_op jit(solution)/shard_map/project/pallas_call | solution.py:51
  66.1 4.2 %collective-permute-done.2 = bf16[48,48,128]{2,0,1:T(8,128)(2,1)S(1)} collective-permute-done((bf16[48,48,128]{2,0,1:T(8,128)(2,1)}, bf16[48,48,128]{2,0,1:T(8,128)(2,1)S(1)}, u32[]{:S(2)}, u32[]{:S(2)}) %collective-permute-start.2) | collective-permute-done | bytes 589856 | tf_op jit(solution)/shard_map/ppermute | solution.py:207
  70.3 0.0 collective-permute-done.3
  70.3 13.8 %collective-permute-done.4 = bf16[48,48,128]{2,0,1:T(8,128)(2,1)S(1)} collective-permute-done((bf16[48,48,128]{2,0,1:T(8,128)(2,1)}, bf16[48,48,128]{2,0,1:T(8,128)(2,1)S(1)}, u32[]{:S(2)}, u32[]{:S(2)}) %collective-permute-start.4) | collective-permute-done | bytes 589856 | tf_op jit(solution)/shard_map/ppermute | solution.py:207
  84.0 0.0 collective-permute-done.5
  84.0 13.7 %collective-permute-done.6 = bf16[48,48,128]{2,0,1:T(8,128)(2,1)} collective-permute-done((bf16[48,48,128]{2,0,1:T(8,128)(2,1)}, bf16[48,48,128]{2,0,1:T(8,128)(2,1)}, u32[]{:S(2)}, u32[]{:S(2)}) %collective-permute-start.6) | collective-permute-done | bytes 589856 | tf_op jit(solution)/shard_map/ppermute | solution.py:207
  97.8 14.3 %all-to-all-start = ((bf16[128,3,3,2,16,128]{5,4,3,2,1,0:T(8,128)(2,1)}), bf16[128,3,3,2,16,128]{5,4,3,2,1,0:T(8,128)(2,1)}, u32[]{:S(2)}, u32[]{:S(2)}) async-start(bf16[128,3,3,2,16,128]{5,4,3,2,1,0:T(8,128)(2,1)} %project.1), calls=%async_computation | async-start | bytes 18874368 | tf_op jit(solution)/shard_map/all_to_all | solution.py:221
  112.0 1.0 copy.22
  113.0 111.5 %all-to-all-done = bf16[128,3,3,2,16,128]{5,4,3,2,1,0:T(8,128)(2,1)} async-done(((bf16[128,3,3,2,16,128]{5,4,3,2,1,0:T(8,128)(2,1)}), bf16[128,3,3,2,16,128]{5,4,3,2,1,0:T(8,128)(2,1)}, u32[]{:S(2)}, u32[]{:S(2)}) %all-to-all-start) | async-done | bytes 9437216 | tf_op jit(solution)/shard_map/all_to_all | solution.py:221
  224.5 7.7 %collective-permute-start.7 = (bf16[48,48,128]{2,0,1:T(8,128)(2,1)}, bf16[48,48,128]{2,0,1:T(8,128)(2,1)S(1)}, u32[]{:S(2)}, u32[]{:S(2)}) collective-permute-start(bf16[48,48,128]{2,0,1:T(8,128)(2,1)} %bitcast.53), channel_id=1, source_target_pairs={{0,28},{1,60},{2,92},{3,124},{4,24},{5,56},{6,88},{7,120},{8,20},{... | collective-permute-start | bytes 1769480 | tf_op jit(solution)/shard_map/ppermute | solution.py:207
  232.1 14.2 %cross.1 = bf16[32,4,3,48,128]{4,3,2,1,0:T(8,128)(2,1)} custom-call(bf16[32,12,3,2,16,128]{5,4,3,2,1,0:T(8,128)(2,1)} %bitcast.10.b_ref.a_ref, bf16[32,12,3,2,16,128]{5,4,3,2,1,0:T(8,128)(2,1)} %bitcast.10.b_ref.a_ref), custom_call_target="tpu_custom_call" | custom-call | flops 7247757312 | bytes 14155776 | tf_op jit(solution)/shard_map/cross/pallas_call | solution.py:98
  246.4 0.0 collective-permute-done.7
  246.4 10.1 %all-to-all-start.1 = ((bf16[128,3,48,128]{3,2,1,0:T(8,128)(2,1)}), bf16[128,3,48,128]{3,2,1,0:T(8,128)(2,1)}, u32[]{:S(2)}, u32[]{:S(2)}) async-start(bf16[128,3,48,128]{3,2,1,0:T(8,128)(2,1)} %bitcast.50), calls=%async_computation.1 | async-start | bytes 9437184 | tf_op jit(solution)/shard_map/all_to_all | solution.py:221
  256.5 1.1 broadcast_in_dim.28
  257.6 0.1 bitcast_dynamic-update-slice_fusion.7
  257.7 0.1 bitcast_dynamic-update-slice_fusion.6
  257.8 0.1 bitcast_dynamic-update-slice_fusion.5
  257.9 0.1 bitcast_dynamic-update-slice_fusion.4
  258.0 0.1 bitcast_dynamic-update-slice_fusion.3
  258.1 1.1 bitcast_dynamic-update-slice_fusion.2
  259.2 1.1 bitcast_dynamic-update-slice_fusion.1
  260.4 0.1 bitcast_dynamic-update-slice_fusion
  260.5 0.0 copy-start
  260.5 2.1 copy-done
  262.6 13.2 %gate.1.g_ref = f32[48,384,128]{2,1,0:T(8,128)} custom-call(bf16[48,384,128]{2,1,0:T(8,128)(2,1)} %bitcast.47, bf16[128,128]{1,0:T(8,128)(2,1)} %w_ref.2), custom_call_target="tpu_custom_call" | custom-call | flops 603979776 | bytes 14155776 | tf_op jit(solution)/shard_map/gate/pallas_call | solution.py:130
  275.7 39.0 %all-to-all-done.1.r_ref = bf16[128,3,48,128]{3,2,1,0:T(8,128)(2,1)} async-done(((bf16[128,3,48,128]{3,2,1,0:T(8,128)(2,1)}), bf16[128,3,48,128]{3,2,1,0:T(8,128)(2,1)}, u32[]{:S(2)}, u32[]{:S(2)}) %all-to-all-start.1) | async-done | bytes 4718624 | tf_op jit(solution)/shard_map/all_to_all | solution.py:221
  314.7 13.7 %finish.1 = bf16[48,384,128]{2,1,0:T(8,128)(2,1)} custom-call(bf16[128,3,48,128]{3,2,1,0:T(8,128)(2,1)} %all-to-all-done.1.r_ref, bf16[48,384,128]{2,1,0:T(8,128)(2,1)} %bitcast.48, f32[48,384,128]{2,1,0:T(8,128)} %gate.1.g_ref, bf16[128,128]{1,0:T(8,128)(2,1)} %w_ref.3), custom_call_target="tpu_custom_call" | custom-call | flops 603979776 | bytes 23592960 | tf_op jit(solution)/shard_map/finish/pallas_call | solution.py:168
Async XLA Ops:
  3.3 40.6 %collective-permute-start = (bf16[48,48,128]{2,0,1:T(8,128)(2,1)S(1)}, bf16[48,48,128]{2,0,1:T(8,128)(2,1)S(1)}, u32[]{:S(2)}, u32[]{:S(2)}) collective-permute-start(bf16[48,48,128]{2,0,1:T(8,128)(2,1)S(1)} %bitcast.52), channel_id=1, source_target_pairs={{0,0},{1,32},{2,64},{3,96},{4,4},{5,36},{6,68},{7,100},{8,8},{9,40... | collective-permute-start | bytes 1769480 | tf_op jit(solution)/shard_map/ppermute | solution.py:207
  8.1 40.3 %collective-permute-start.1 = (bf16[48,48,128]{2,0,1:T(8,128)(2,1)S(1)}, bf16[48,48,128]{2,0,1:T(8,128)(2,1)S(1)}, u32[]{:S(2)}, u32[]{:S(2)}) collective-permute-start(bf16[48,48,128]{2,0,1:T(8,128)(2,1)S(1)} %bitcast.51), channel_id=1, source_target_pairs={{0,4},{1,36},{2,68},{3,100},{4,0},{5,32},{6,64},{7,96},{8,12},{9,4... | collective-permute-start | bytes 1769480 | tf_op jit(solution)/shard_map/ppermute | solution.py:207
  10.1 60.2 %collective-permute-start.2 = (bf16[48,48,128]{2,0,1:T(8,128)(2,1)}, bf16[48,48,128]{2,0,1:T(8,128)(2,1)S(1)}, u32[]{:S(2)}, u32[]{:S(2)}) collective-permute-start(bf16[48,48,128]{2,0,1:T(8,128)(2,1)} %bitcast.44), channel_id=1, source_target_pairs={{0,8},{1,40},{2,72},{3,104},{4,12},{5,44},{6,76},{7,108},{8,0},{9,... | collective-permute-start | bytes 1769480 | tf_op jit(solution)/shard_map/ppermute | solution.py:207
  14.1 56.1 %collective-permute-start.3 = (bf16[48,48,128]{2,0,1:T(8,128)(2,1)}, bf16[48,48,128]{2,0,1:T(8,128)(2,1)S(1)}, u32[]{:S(2)}, u32[]{:S(2)}) collective-permute-start(bf16[48,48,128]{2,0,1:T(8,128)(2,1)} %bitcast.43), channel_id=1, source_target_pairs={{0,12},{1,44},{2,76},{3,108},{4,8},{5,40},{6,72},{7,104},{8,4},{9,... | collective-permute-start | bytes 1769480 | tf_op jit(solution)/shard_map/ppermute | solution.py:207
  15.1 68.9 %collective-permute-start.4 = (bf16[48,48,128]{2,0,1:T(8,128)(2,1)}, bf16[48,48,128]{2,0,1:T(8,128)(2,1)S(1)}, u32[]{:S(2)}, u32[]{:S(2)}) collective-permute-start(bf16[48,48,128]{2,0,1:T(8,128)(2,1)} %bitcast.42), channel_id=1, source_target_pairs={{0,16},{1,48},{2,80},{3,112},{4,20},{5,52},{6,84},{7,116},{8,24},{... | collective-permute-start | bytes 1769480 | tf_op jit(solution)/shard_map/ppermute | solution.py:207
  43.9 40.1 %collective-permute-start.5 = (bf16[48,48,128]{2,0,1:T(8,128)(2,1)}, bf16[48,48,128]{2,0,1:T(8,128)(2,1)}, u32[]{:S(2)}, u32[]{:S(2)}) collective-permute-start(bf16[48,48,128]{2,0,1:T(8,128)(2,1)} %bitcast.41), channel_id=1, source_target_pairs={{0,20},{1,52},{2,84},{3,116},{4,16},{5,48},{6,80},{7,112},{8,28},{... | collective-permute-start | bytes 1769480 | tf_op jit(solution)/shard_map/ppermute | solution.py:207
  48.4 49.4 %collective-permute-start.6 = (bf16[48,48,128]{2,0,1:T(8,128)(2,1)}, bf16[48,48,128]{2,0,1:T(8,128)(2,1)}, u32[]{:S(2)}, u32[]{:S(2)}) collective-permute-start(bf16[48,48,128]{2,0,1:T(8,128)(2,1)} %bitcast.40), channel_id=1, source_target_pairs={{0,24},{1,56},{2,88},{3,120},{4,28},{5,60},{6,92},{7,124},{8,16},{... | collective-permute-start | bytes 1769480 | tf_op jit(solution)/shard_map/ppermute | solution.py:207
  97.8 126.7 %all-to-all-start = ((bf16[128,3,3,2,16,128]{5,4,3,2,1,0:T(8,128)(2,1)}), bf16[128,3,3,2,16,128]{5,4,3,2,1,0:T(8,128)(2,1)}, u32[]{:S(2)}, u32[]{:S(2)}) async-start(bf16[128,3,3,2,16,128]{5,4,3,2,1,0:T(8,128)(2,1)} %project.1), calls=%async_computation | async-start | bytes 18874368 | tf_op jit(solution)/shard_map/all_to_all | solution.py:221
  224.5 21.9 %collective-permute-start.7 = (bf16[48,48,128]{2,0,1:T(8,128)(2,1)}, bf16[48,48,128]{2,0,1:T(8,128)(2,1)S(1)}, u32[]{:S(2)}, u32[]{:S(2)}) collective-permute-start(bf16[48,48,128]{2,0,1:T(8,128)(2,1)} %bitcast.53), channel_id=1, source_target_pairs={{0,28},{1,60},{2,92},{3,124},{4,24},{5,56},{6,88},{7,120},{8,20},{... | collective-permute-start | bytes 1769480 | tf_op jit(solution)/shard_map/ppermute | solution.py:207
  246.4 68.4 %all-to-all-start.1 = ((bf16[128,3,48,128]{3,2,1,0:T(8,128)(2,1)}), bf16[128,3,48,128]{3,2,1,0:T(8,128)(2,1)}, u32[]{:S(2)}, u32[]{:S(2)}) async-start(bf16[128,3,48,128]{3,2,1,0:T(8,128)(2,1)} %bitcast.50), calls=%async_computation.1 | async-start | bytes 9437184 | tf_op jit(solution)/shard_map/all_to_all | solution.py:221
  260.5 2.1 copy-start

commit v3 on v2

--- a/solution.py
+++ b/solution.py
@@ -7,16 +7,14 @@
 
 ALL = ("row", "col")
 GB = 16
-EARLY = 7
-VMEM_LIMIT = 56 * 1024 * 1024
 
 
 def sigmoid(x):
     return 0.5 * jnp.tanh(0.5 * x) + 0.5
 
 
-def params():
-    return pltpu.CompilerParams(vmem_limit_bytes=VMEM_LIMIT)
+def params(mib):
+    return pltpu.CompilerParams(vmem_limit_bytes=mib * 1024 * 1024)
 
 
 def project_kernel(x_ref, wt_ref, o_ref, sa, sb):
@@ -58,7 +56,7 @@
         out_specs=pl.BlockSpec((hidden, None, None, 2, GB, 128), lambda k, i: (0, k, i, 0, 0, 0)),
         out_shape=jax.ShapeDtypeStruct((hidden, kg, rows // GB, 2, GB, 128), jnp.bfloat16),
         scratch_shapes=[pltpu.VMEM((hidden * GB, 128), jnp.float32)] * 2,
-        compiler_params=params(),
+        compiler_params=params(16),
         cost_estimate=pl.CostEstimate(
             flops=2 * rows * cols * width * hidden * 4,
             bytes_accessed=6 * rows * cols * width,
@@ -104,7 +102,7 @@
         ],
         out_specs=pl.BlockSpec((nb, col_count, kg, rows, 128), lambda j: (j, 0, 0, 0, 0)),
         out_shape=jax.ShapeDtypeStruct((row_count, col_count, kg, rows, 128), jnp.bfloat16),
-        compiler_params=params(),
+        compiler_params=params(56),
         cost_estimate=pl.CostEstimate(
             flops=2 * tokens**3, bytes_accessed=6 * tokens * tokens, transcendentals=0
         ),
@@ -119,9 +117,8 @@
     z = z - mean
     var = jnp.mean(z * z, axis=-1, keepdims=True)
     n = (z * lax.rsqrt(var + 1e-5)).astype(jnp.bfloat16)
-    g_ref[...] = sigmoid(
-        jnp.dot(n, w_ref[...], preferred_element_type=jnp.float32)
-    ).reshape(g_ref.shape)
+    gate = sigmoid(jnp.dot(n, w_ref[...], preferred_element_type=jnp.float32))
+    g_ref[...] = gate.astype(g_ref.dtype).reshape(g_ref.shape)
 
 
 def gate_of(z, w_gate):
@@ -135,8 +132,8 @@
             pl.BlockSpec((width, width), lambda j: (0, 0)),
         ],
         out_specs=pl.BlockSpec((jb, cols, width), lambda j: (j, 0, 0)),
-        out_shape=jax.ShapeDtypeStruct((rows, cols, width), jnp.float32),
-        compiler_params=params(),
+        out_shape=jax.ShapeDtypeStruct((rows, cols, width), jnp.bfloat16),
+        compiler_params=params(12),
         cost_estimate=pl.CostEstimate(
             flops=2 * rows * cols * width * width,
             bytes_accessed=6 * rows * cols * width,
@@ -148,17 +145,25 @@
 
 def finish_kernel(r_ref, z_ref, g_ref, w_ref, o_ref, scr):
     hidden, jb, _ = r_ref.shape
+    width = w_ref.shape[1]
+    batch = 4
     scr[...] = r_ref[...].astype(jnp.float32).reshape(hidden * jb, 128)
-    for j in range(jb):
-        v = scr[pl.ds(j, hidden, stride=jb), :]
-        mean = jnp.mean(v, axis=0, keepdims=True)
-        v = v - mean
-        var = jnp.mean(v * v, axis=0, keepdims=True)
-        n = (v * lax.rsqrt(var + 1e-5)).astype(jnp.bfloat16)
+    for first in range(0, jb, batch):
+        parts = []
+        for j in range(first, first + batch):
+            v = scr[pl.ds(j, hidden, stride=jb), :]
+            mean = jnp.mean(v, axis=0, keepdims=True)
+            v = v - mean
+            var = jnp.mean(v * v, axis=0, keepdims=True)
+            parts.append((v * lax.rsqrt(var + 1e-5)).astype(jnp.bfloat16))
         update = lax.dot_general(
-            n, w_ref[...], (((0,), (0,)), ((), ())), preferred_element_type=jnp.float32
-        )
-        o_ref[j] = (z_ref[j].astype(jnp.float32) + g_ref[j] * update).astype(jnp.bfloat16)
+            jnp.concatenate(parts, axis=1),
+            w_ref[...],
+            (((0,), (0,)), ((), ())),
+            preferred_element_type=jnp.float32,
+        ).reshape(batch, 128, width)
+        at = pl.ds(first, batch)
+        o_ref[at] = (z_ref[at].astype(jnp.float32) + g_ref[at].astype(jnp.float32) * update).astype(jnp.bfloat16)
 
 
 def finish(returned, z, gate, w_out):
@@ -177,7 +182,7 @@
         out_specs=tok,
         out_shape=jax.ShapeDtypeStruct((rows, cols, width), jnp.bfloat16),
         scratch_shapes=[pltpu.VMEM((hidden * GB, 128), jnp.float32)],
-        compiler_params=params(),
+        compiler_params=params(56),
         cost_estimate=pl.CostEstimate(
             flops=2 * rows * cols * width * hidden,
             bytes_accessed=10 * rows * cols * width,
@@ -197,14 +202,35 @@
     ]
 
 
-def send(piece, s, low, high):
-    perm = [
-        ((h * low + q) * high + c, (c * low + (q ^ s)) * high + h)
-        for h in range(high)
-        for q in range(low)
-        for c in range(high)
-    ]
+def send(piece, low, high, target, chosen=lambda h, q, c: True):
+    perm = []
+    for h in range(high):
+        for q in range(low):
+            for c in range(high):
+                if chosen(h, q, c):
+                    th, tq, tc = target(h, q, c)
+                    perm.append(((h * low + q) * high + c, (th * low + tq) * high + tc))
     return lax.ppermute(piece, ALL, perm)
+
+
+def near(h, q, c):
+    return h // 2 == c // 2
+
+
+def far(h, q, c):
+    return not near(h, q, c)
+
+
+def final(s):
+    return lambda h, q, c: (c, q ^ s, h)
+
+
+def halfway(s):
+    return lambda h, q, c: (c, q ^ s, c // 2 * 2 + h % 2)
+
+
+def onward(h, q, c):
+    return h, q, c ^ 2
 
 
 def place(moved):
@@ -223,17 +249,40 @@
 
 def on_device(pair, w_in, w_gate, w_out):
     row_count = lax.axis_size("row")
-    col_count = lax.axis_size("col")
-    low = row_count // col_count
-    pieces = cut(pair, low)
-    early = [send(pieces[s], s, low, col_count) for s in range(EARLY)]
-    early, both = lax.optimization_barrier((early, project(pair, w_in)))
+    high = lax.axis_size("col")
+    low = row_count // high
+    rows = pair.shape[0]
+    is_far = lax.axis_index("row") // low // 2 != lax.axis_index("col") // 2
+    p = cut(pair, low)
+
+    def direct(s, piece):
+        return send(piece, low, high, final(s))
+
+    def inner(s, piece):
+        return send(piece, low, high, final(s), near)
+
+    def first_leg(s, piece):
+        return send(piece, low, high, halfway(s), far)
+
+    def second_leg(piece):
+        return send(piece, low, high, onward, near)
+
+    half0, half1 = first_leg(0, p[0]), first_leg(1, p[1])
+    got = {s: direct(s, p[s]) for s in (2, 3, 4)}
+    half0, half1, p0, p1, p5, p6, p7 = lax.optimization_barrier((half0, half1, p[0], p[1], p[5], p[6], p[7]))
+    leg = second_leg(jnp.concatenate([half0, half1], axis=0))
+    got[5], got[6] = direct(5, p5), direct(6, p6)
+    in0, in1 = inner(0, p0), inner(1, p1)
+    got, leg, in0, in1, p7, both = lax.optimization_barrier(
+        (got, leg, in0, in1, p7, project(pair, w_in))
+    )
     own = exchange(both)
-    own, rest = lax.optimization_barrier((own, pieces[EARLY:]))
-    late = [send(p, EARLY + s, low, col_count) for s, p in enumerate(rest)]
-    late, crossed = lax.optimization_barrier((late, cross(own, row_count, col_count)))
+    own, p7 = lax.optimization_barrier((own, p7))
+    got[7], crossed = lax.optimization_barrier((direct(7, p7), cross(own, row_count, high)))
     returned = exchange(crossed)
-    turned = place(early + late)
+    got[0] = jnp.where(is_far, leg[:rows], in0)
+    got[1] = jnp.where(is_far, leg[rows:], in1)
+    turned = place([got[s] for s in range(low)])
     return finish(returned, turned, gate_of(turned, w_gate), w_out)
 
 

time: 330 us -> 310 us (0.939)
  waiting for transfers between devices: 204 us -> 81.7 us
  blocking collectives: 0 us -> 118 us
  starting transfers between devices: 51.5 us -> 39.2 us
  Pallas kernels: 55.5 us -> 47.9 us
    all_to_all x0 -> x1, blocking collectives: none -> 118 us  [exchange(): return lax.all_to_all(x, ALL, split_axis=0, concat_axis=0, tiled=True)]
    all_to_all x2 -> x1, waiting for transfers between devices: 150 us -> 40.4 us  [exchange(): return lax.all_to_all(x, ALL, split_axis=0, concat_axis=0, tiled=True)]
    all_to_all x2 -> x1, starting transfers between devices: 24.4 us -> 6.92 us  [exchange(): return lax.all_to_all(x, ALL, split_axis=0, concat_axis=0, tiled=True)]
    ppermute x8 -> x11, waiting for transfers between devices: 53.9 us -> 41.4 us  [send(): return lax.ppermute(piece, ALL, perm)]
    ppermute x8 -> x11, starting transfers between devices: 27.1 us -> 32.3 us  [send(): return lax.ppermute(piece, ALL, perm)]
    pallas_call x1, Pallas kernels: 13.2 us -> 8.03 us  [gate_of(): pl.pallas_call(gate_kernel, grid=(rows // jb,), in_specs=[pl.BlockSpec((j...]
    unnamed x3 -> x29, local copies, waits for them, and re-layouts: 3.76 us -> 8.57 us
    dynamic_slice x9 -> x7, local copies, waits for them, and re-layouts: 9.3 us -> 6.6 us  [cut(): lax.dynamic_index_in_dim(pieces, lax.bitwise_xor(me, s), 1, keepdims=False)]
  transfers between devices with their start and end apart: 10 -> 12, of which waited for: 6 -> 6; matrix products, arithmetic and copies ran while one was open for 4% -> 3% of each run, Pallas kernels for 13% -> 11%
where the time goes in v3:
time: 310 us; the launch traced here: 309 us
  blocking collectives  118 us (38%)
  waiting for transfers between devices  81.7 us (26%)
  Pallas kernels  47.9 us (15%)
  starting transfers between devices  39.2 us (13%)
  local copies, waits for them, and re-layouts  20.2 us (7%)
    all_to_all x1, blocking collectives, exchange(): return lax.all_to_all(x, ALL, split_axis=0, concat_axis=0, tiled=True)  118 us
    ppermute x11, waiting for transfers between devices, send(): return lax.ppermute(piece, ALL, perm)  41.4 us
    all_to_all x1, waiting for transfers between devices, exchange(): return lax.all_to_all(x, ALL, split_axis=0, concat_axis=0, tiled=True)  40.4 us
    ppermute x11, starting transfers between devices, send(): return lax.ppermute(piece, ALL, perm)  32.3 us
    pallas_call x1, Pallas kernels, cross(): pl.pallas_call(cross_kernel, grid=(row_count // nb,), in_specs=[pl.BlockS...  14.2 us
    pallas_call x1, Pallas kernels, project(): pl.pallas_call(project_kernel, grid=(kg, rows // GB), in_specs=[pl.BlockS...  12.9 us
    pallas_call x1, Pallas kernels, finish(): pl.pallas_call(finish_kernel, grid=(rows // GB, groups), in_specs=[pl.Blo...  12.8 us
    unnamed x29, local copies, waits for them, and re-layouts  8.57 us
  transfers between devices with their start and end apart: 12, of which 6 were waited for; matrix products, arithmetic and copies ran while one was open for 3% of the time, Pallas kernels for 11%

profile of v3, /device:TPU:1, one launch (start us, length us, event | category | flops | bytes accessed | tf_op | source)
XLA Modules:
  0.0 309.2 jit_solution(12951840026596311365)
XLA Ops:
  0.0 3.2 %constant_dynamic-slice_fusion = (bf16[48,1,48,128]{3,2,1,0:T(8,128)(2,1)S(1)}, bf16[48,1,48,128]{3,2,1,0:T(8,128)(2,1)S(1)}, bf16[48,1,48,128]{3,2,1,0:T(8,128)...) fusion(bf16[48,8,48,128]{3,2,1,0:T(8,128)(2,1)} %bitcast.49, ...), kind=kLoop, calls=%fused_computation.17 | loop fusion | bytes 9437216 | tf_op jit(solution)/shard_map/jit(dynamic_index_in_dim)/dynamic_slice | solution.py:200
  3.2 1.0 copy.25
  4.2 1.3 collective-permute-start.3
  5.5 1.0 copy.24
  6.5 1.3 collective-permute-start.4
  7.7 0.0 copy-start.13
  7.8 0.2 copy.28
  7.9 4.1 %collective-permute-start = (bf16[48,48,128]{2,0,1:T(8,128)(2,1)S(1)}, bf16[48,48,128]{2,0,1:T(8,128)(2,1)S(1)}, u32[]{:S(2)}, u32[]{:S(2)}) collective-permute-start(bf16[48,48,128]{2,0,1:T(8,128)(2,1)S(1)} %bitcast.56), channel_id=1, source_target_pairs={{0,8},{1,40},{2,72},{3,104},{4,12},{5,44},{6,76},{7,108},{8,0},{9,... | collective-permute-start | bytes 1769480 | tf_op jit(solution)/shard_map/ppermute | solution.py:213
  12.0 0.2 copy.27
  12.2 1.0 collective-permute-start.1
  13.2 0.2 copy.26
  13.4 4.7 %collective-permute-start.2 = (bf16[48,48,128]{2,0,1:T(8,128)(2,1)S(1)}, bf16[48,48,128]{2,0,1:T(8,128)(2,1)S(1)}, u32[]{:S(2)}, u32[]{:S(2)}) collective-permute-start(bf16[48,48,128]{2,0,1:T(8,128)(2,1)S(1)} %bitcast.54), channel_id=1, source_target_pairs={{0,16},{1,48},{2,80},{3,112},{4,20},{5,52},{6,84},{7,116},{8,24},{... | collective-permute-start | bytes 1769480 | tf_op jit(solution)/shard_map/ppermute | solution.py:213
  18.0 1.0 copy.23
  19.0 1.3 copy_bitcast_fusion
  20.4 15.9 %collective-permute-done.3 = bf16[48,48,128]{2,0,1:T(8,128)(2,1)S(1)} collective-permute-done((bf16[48,48,128]{2,0,1:T(8,128)(2,1)}, bf16[48,48,128]{2,0,1:T(8,128)(2,1)S(1)}, u32[]{:S(2)}, u32[]{:S(2)}) %collective-permute-start.3) | collective-permute-done | bytes 589856 | tf_op jit(solution)/shard_map/ppermute | solution.py:213
  36.3 0.0 collective-permute-done.4
  36.3 0.1 pad_maximum_fusion
  36.4 4.4 %collective-permute-start.7 = (bf16[96,48,128]{2,0,1:T(8,128)(2,1)S(1)}, bf16[96,48,128]{2,0,1:T(8,128)(2,1)S(1)}, u32[]{:S(2)}, u32[]{:S(2)}) collective-permute-start(bf16[96,48,128]{2,0,1:T(8,128)(2,1)S(1)} %pad_maximum_fusion), channel_id=1, source_target_pairs={{0,2},{1,3},{4,6},{5,7},{8,10},{9,11},{12,14},{13,15},{16,18},{17,... | collective-permute-start | bytes 3538952 | tf_op jit(solution)/shard_map/ppermute | solution.py:213
  40.8 4.1 %collective-permute-start.5 = (bf16[48,48,128]{2,0,1:T(8,128)(2,1)}, bf16[48,48,128]{2,0,1:T(8,128)(2,1)}, u32[]{:S(2)}, u32[]{:S(2)}) collective-permute-start(bf16[48,48,128]{2,0,1:T(8,128)(2,1)} %bitcast.41), channel_id=1, source_target_pairs={{0,20},{1,52},{2,84},{3,116},{4,16},{5,48},{6,80},{7,112},{8,28},{... | collective-permute-start | bytes 1769480 | tf_op jit(solution)/shard_map/ppermute | solution.py:213
  45.0 0.0 collective-permute-done
  45.0 1.2 collective-permute-start.6
  46.2 0.0 collective-permute-done.1
  46.2 2.6 collective-permute-start.8
  48.8 2.7 collective-permute-done.2
  51.5 0.0 copy-done.4
  51.5 0.0 copy-done.6
  51.5 0.8 copy-done.8
  52.3 6.3 %collective-permute-start.9 = (bf16[48,48,128]{2,0,1:T(8,128)(2,1)}, bf16[48,48,128]{2,0,1:T(8,128)(2,1)}, u32[]{:S(2)}, u32[]{:S(2)}) collective-permute-start(bf16[48,48,128]{2,0,1:T(8,128)(2,1)} %bitcast.42), channel_id=1, source_target_pairs={{0,4},{1,36},{4,0},{5,32},{8,12},{9,44},{12,8},{13,40},{16,20},{17... | collective-permute-start | bytes 1769480 | tf_op jit(solution)/shard_map/ppermute | solution.py:213
  58.6 0.0 copy-done.13
  58.6 0.1 copy.13
  58.7 0.0 copy-start.1
  58.8 2.3 copy-done.1
  61.1 12.9 %project.1 = bf16[128,3,3,2,16,128]{5,4,3,2,1,0:T(8,128)(2,1)S(1)} custom-call(bf16[48,384,128]{2,1,0:T(8,128)(2,1)S(1)} %copy-done.1, bf16[512,128]{1,0:T(8,128)(2,1)S(1)} %bitcast.50), custom_call_target="tpu_custom_call" | custom-call | flops 2415919104 | bytes 14155776 | tf_op jit(solution)/shard_map/project/pallas_call | solution.py:49
  73.9 0.0 copy-start.12
  74.0 10.6 %collective-permute-done.5 = bf16[48,48,128]{2,0,1:T(8,128)(2,1)} collective-permute-done((bf16[48,48,128]{2,0,1:T(8,128)(2,1)}, bf16[48,48,128]{2,0,1:T(8,128)(2,1)}, u32[]{:S(2)}, u32[]{:S(2)}) %collective-permute-start.5) | collective-permute-done | bytes 589856 | tf_op jit(solution)/shard_map/ppermute | solution.py:213
  84.6 0.0 collective-permute-done.6
  84.6 9.0 %collective-permute-done.8 = bf16[48,48,128]{2,0,1:T(8,128)(2,1)S(1)} collective-permute-done((bf16[48,48,128]{2,0,1:T(8,128)(2,1)}, bf16[48,48,128]{2,0,1:T(8,128)(2,1)S(1)}, u32[]{:S(2)}, u32[]{:S(2)}) %collective-permute-start.8) | collective-permute-done | bytes 589856 | tf_op jit(solution)/shard_map/ppermute | solution.py:213
  93.6 0.0 collective-permute-done.9
  93.6 0.0 collective-permute-done.7
  93.6 118.2 %all_to_all.10 = bf16[128,3,3,2,16,128]{5,4,3,2,1,0:T(8,128)(2,1)} all-to-all(bf16[128,3,3,2,16,128]{5,4,3,2,1,0:T(8,128)(2,1)S(1)} %project.1), channel_id=1, replica_groups=mesh['row'=32,'col'=4] {'row','col'}, dimensions={0} | all-to-all | bytes 18874368 | tf_op jit(solution)/shard_map/all_to_all | solution.py:247
  211.9 0.0 copy-done.12
  211.9 1.3 collective-permute-start.10
  213.1 14.2 %cross.1 = bf16[32,4,3,48,128]{4,3,2,1,0:T(8,128)(2,1)} custom-call(bf16[32,12,3,2,16,128]{5,4,3,2,1,0:T(8,128)(2,1)} %bitcast.51, bf16[32,12,3,2,16,128]{5,4,3,2,1,0:T(8,128)(2,1)} %bitcast.52), custom_call_target="tpu_custom_call" | custom-call | flops 7247757312 | bytes 14155776 | tf_op jit(solution)/shard_map/cross/pallas_call | solution.py:96
  227.4 3.0 collective-permute-done.10
  230.4 0.9 copy-done.10
  231.2 6.9 %all-to-all-start.1 = ((bf16[128,3,48,128]{3,2,1,0:T(8,128)(2,1)}), bf16[128,3,48,128]{3,2,1,0:T(8,128)(2,1)}, u32[]{:S(2)}, u32[]{:S(2)}) async-start(bf16[128,3,48,128]{3,2,1,0:T(8,128)(2,1)} %bitcast.53), calls=%async_computation.1 | async-start | bytes 9437184 | tf_op jit(solution)/shard_map/all_to_all | solution.py:247
  238.2 0.0 copy-start.5
  238.2 0.0 copy-start.7
  238.3 1.1 broadcast_in_dim.28
  239.4 0.2 bitcast_dynamic-update-slice_fusion
  239.6 0.0 copy-start.3
  239.6 1.3 bitcast_dynamic-update-slice_fusion.7
  240.9 0.0 copy-done.5
  240.9 0.1 bitcast_dynamic-update-slice_fusion.6
  241.0 0.1 bitcast_dynamic-update-slice_fusion.5
  241.1 0.1 bitcast_dynamic-update-slice_fusion.4
  241.2 1.1 bitcast_dynamic-update-slice_fusion.3
  242.3 1.1 bitcast_dynamic-update-slice_fusion.2
  243.5 0.1 bitcast_dynamic-update-slice_fusion.1
  243.6 8.0 %gate.1.g_ref = bf16[48,384,128]{2,1,0:T(8,128)(2,1)S(1)} custom-call(bf16[48,384,128]{2,1,0:T(8,128)(2,1)S(1)} %bitcast.47, bf16[128,128]{1,0:T(8,128)(2,1)S(1)} %copy-done.3), custom_call_target="tpu_custom_call" | custom-call | flops 603979776 | bytes 14155776 | tf_op jit(solution)/shard_map/gate/pallas_call | solution.py:127
  251.6 2.2 copy-done
  253.8 2.2 copy-done.2
  256.0 40.4 %all-to-all-done.1.r_ref = bf16[128,3,48,128]{3,2,1,0:T(8,128)(2,1)} async-done(((bf16[128,3,48,128]{3,2,1,0:T(8,128)(2,1)}), bf16[128,3,48,128]{3,2,1,0:T(8,128)(2,1)}, u32[]{:S(2)}, u32[]{:S(2)}) %all-to-all-start.1) | async-done | bytes 4718624 | tf_op jit(solution)/shard_map/all_to_all | solution.py:247
  296.4 12.8 %finish.1 = bf16[48,384,128]{2,1,0:T(8,128)(2,1)} custom-call(bf16[128,3,48,128]{3,2,1,0:T(8,128)(2,1)} %all-to-all-done.1.r_ref, bf16[48,384,128]{2,1,0:T(8,128)(2,1)} %bitcast.48, bf16[48,384,128]{2,1,0:T(8,128)(2,1)} %copy-done.2, bf16[128,128]{1,0:T(8,128)(2,1)} %w_ref.3), custom_call_target="tpu_custom_call" | custom-call | flops 603979776 | bytes 23592960 | tf_op jit(solution)/shard_map/finish/pallas_call | solution.py:173
  (12 shorter events, 0.0 us)
Async XLA Ops:
  4.2 32.1 %collective-permute-start.3 = (bf16[48,48,128]{2,0,1:T(8,128)(2,1)}, bf16[48,48,128]{2,0,1:T(8,128)(2,1)S(1)}, u32[]{:S(2)}, u32[]{:S(2)}) collective-permute-start(bf16[48,48,128]{2,0,1:T(8,128)(2,1)} %bitcast.43), channel_id=1, source_target_pairs={{2,66},{3,98},{6,70},{7,102},{10,74},{11,106},{14,78},{15,110},{18... | collective-permute-start | bytes 1769480 | tf_op jit(solution)/shard_map/ppermute | solution.py:213
  6.5 29.8 %collective-permute-start.4 = (bf16[48,48,128]{2,0,1:T(8,128)(2,1)}, bf16[48,48,128]{2,0,1:T(8,128)(2,1)S(1)}, u32[]{:S(2)}, u32[]{:S(2)}) collective-permute-start(bf16[48,48,128]{2,0,1:T(8,128)(2,1)} %bitcast.42), channel_id=1, source_target_pairs={{2,70},{3,102},{6,66},{7,98},{10,78},{11,110},{14,74},{15,106},{18... | collective-permute-start | bytes 1769480 | tf_op jit(solution)/shard_map/ppermute | solution.py:213
  7.7 50.9 %copy-start.13 = (bf16[128,512]{1,0:T(8,128)(2,1)S(1)}, bf16[128,512]{1,0:T(8,128)(2,1)}, u32[]{:S(2)}) copy-start(bf16[128,512]{1,0:T(8,128)(2,1)} %param.5) | copy-start | bytes 393220
  7.9 37.0 %collective-permute-start = (bf16[48,48,128]{2,0,1:T(8,128)(2,1)S(1)}, bf16[48,48,128]{2,0,1:T(8,128)(2,1)S(1)}, u32[]{:S(2)}, u32[]{:S(2)}) collective-permute-start(bf16[48,48,128]{2,0,1:T(8,128)(2,1)S(1)} %bitcast.56), channel_id=1, source_target_pairs={{0,8},{1,40},{2,72},{3,104},{4,12},{5,44},{6,76},{7,108},{8,0},{9,... | collective-permute-start | bytes 1769480 | tf_op jit(solution)/shard_map/ppermute | solution.py:213
  12.2 34.0 %collective-permute-start.1 = (bf16[48,48,128]{2,0,1:T(8,128)(2,1)S(1)}, bf16[48,48,128]{2,0,1:T(8,128)(2,1)S(1)}, u32[]{:S(2)}, u32[]{:S(2)}) collective-permute-start(bf16[48,48,128]{2,0,1:T(8,128)(2,1)S(1)} %bitcast.55), channel_id=1, source_target_pairs={{0,12},{1,44},{2,76},{3,108},{4,8},{5,40},{6,72},{7,104},{8,4},{9,... | collective-permute-start | bytes 1769480 | tf_op jit(solution)/shard_map/ppermute | solution.py:213
  13.4 38.1 %collective-permute-start.2 = (bf16[48,48,128]{2,0,1:T(8,128)(2,1)S(1)}, bf16[48,48,128]{2,0,1:T(8,128)(2,1)S(1)}, u32[]{:S(2)}, u32[]{:S(2)}) collective-permute-start(bf16[48,48,128]{2,0,1:T(8,128)(2,1)S(1)} %bitcast.54), channel_id=1, source_target_pairs={{0,16},{1,48},{2,80},{3,112},{4,20},{5,52},{6,84},{7,116},{8,24},{... | collective-permute-start | bytes 1769480 | tf_op jit(solution)/shard_map/ppermute | solution.py:213
  36.4 57.3 %collective-permute-start.7 = (bf16[96,48,128]{2,0,1:T(8,128)(2,1)S(1)}, bf16[96,48,128]{2,0,1:T(8,128)(2,1)S(1)}, u32[]{:S(2)}, u32[]{:S(2)}) collective-permute-start(bf16[96,48,128]{2,0,1:T(8,128)(2,1)S(1)} %pad_maximum_fusion), channel_id=1, source_target_pairs={{0,2},{1,3},{4,6},{5,7},{8,10},{9,11},{12,14},{13,15},{16,18},{17,... | collective-permute-start | bytes 3538952 | tf_op jit(solution)/shard_map/ppermute | solution.py:213
  40.8 43.8 %collective-permute-start.5 = (bf16[48,48,128]{2,0,1:T(8,128)(2,1)}, bf16[48,48,128]{2,0,1:T(8,128)(2,1)}, u32[]{:S(2)}, u32[]{:S(2)}) collective-permute-start(bf16[48,48,128]{2,0,1:T(8,128)(2,1)} %bitcast.41), channel_id=1, source_target_pairs={{0,20},{1,52},{2,84},{3,116},{4,16},{5,48},{6,80},{7,112},{8,28},{... | collective-permute-start | bytes 1769480 | tf_op jit(solution)/shard_map/ppermute | solution.py:213
  45.0 6.5 %copy-start.4 = (bf16[48,48,128]{2,0,1:T(8,128)(2,1)}, bf16[48,48,128]{2,0,1:T(8,128)(2,1)S(1)}, u32[]{:S(2)}) copy-start(bf16[48,48,128]{2,0,1:T(8,128)(2,1)S(1)} %collective-permute-done) | copy-start | bytes 1769476
  45.0 39.6 %collective-permute-start.6 = (bf16[48,48,128]{2,0,1:T(8,128)(2,1)}, bf16[48,48,128]{2,0,1:T(8,128)(2,1)}, u32[]{:S(2)}, u32[]{:S(2)}) collective-permute-start(bf16[48,48,128]{2,0,1:T(8,128)(2,1)} %get-tuple-element.27), channel_id=1, source_target_pairs={{0,24},{1,56},{2,88},{3,120},{4,28},{5,60},{6,92},{7,124},{8,16},{... | collective-permute-start | bytes 1769480 | tf_op jit(solution)/shard_map/ppermute | solution.py:213
  46.2 5.3 %copy-start.6 = (bf16[48,48,128]{2,0,1:T(8,128)(2,1)}, bf16[48,48,128]{2,0,1:T(8,128)(2,1)S(1)}, u32[]{:S(2)}) copy-start(bf16[48,48,128]{2,0,1:T(8,128)(2,1)S(1)} %collective-permute-done.1) | copy-start | bytes 1769476
  46.2 47.5 %collective-permute-start.8 = (bf16[48,48,128]{2,0,1:T(8,128)(2,1)}, bf16[48,48,128]{2,0,1:T(8,128)(2,1)S(1)}, u32[]{:S(2)}, u32[]{:S(2)}) collective-permute-start(bf16[48,48,128]{2,0,1:T(8,128)(2,1)} %bitcast.43), channel_id=1, source_target_pairs={{0,0},{1,32},{4,4},{5,36},{8,8},{9,40},{12,12},{13,44},{16,16},{17... | collective-permute-start | bytes 1769480 | tf_op jit(solution)/shard_map/ppermute | solution.py:213
  51.5 0.8 copy-start.8
  52.3 41.3 %collective-permute-start.9 = (bf16[48,48,128]{2,0,1:T(8,128)(2,1)}, bf16[48,48,128]{2,0,1:T(8,128)(2,1)}, u32[]{:S(2)}, u32[]{:S(2)}) collective-permute-start(bf16[48,48,128]{2,0,1:T(8,128)(2,1)} %bitcast.42), channel_id=1, source_target_pairs={{0,4},{1,36},{4,0},{5,32},{8,12},{9,44},{12,8},{13,40},{16,20},{17... | collective-permute-start | bytes 1769480 | tf_op jit(solution)/shard_map/ppermute | solution.py:213
  58.7 2.3 copy-start.1
  73.9 137.9 %copy-start.12 = (bf16[48,48,128]{2,0,1:T(8,128)(2,1)S(1)}, bf16[48,48,128]{2,0,1:T(8,128)(2,1)}, u32[]{:S(2)}) copy-start(bf16[48,48,128]{2,0,1:T(8,128)(2,1)} %get-tuple-element.35) | copy-start | bytes 1769476
  211.9 18.5 %collective-permute-start.10 = (bf16[48,48,128]{2,0,1:T(8,128)(2,1)S(1)}, bf16[48,48,128]{2,0,1:T(8,128)(2,1)S(1)}, u32[]{:S(2)}, u32[]{:S(2)}) collective-permute-start(bf16[48,48,128]{2,0,1:T(8,128)(2,1)S(1)} %copy-done.12), channel_id=1, source_target_pairs={{0,28},{1,60},{2,92},{3,124},{4,24},{5,56},{6,88},{7,120},{8,20},{... | collective-permute-start | bytes 1769480 | tf_op jit(solution)/shard_map/ppermute | solution.py:213
  230.4 0.9 copy-start.10
  231.2 65.2 %all-to-all-start.1 = ((bf16[128,3,48,128]{3,2,1,0:T(8,128)(2,1)}), bf16[128,3,48,128]{3,2,1,0:T(8,128)(2,1)}, u32[]{:S(2)}, u32[]{:S(2)}) async-start(bf16[128,3,48,128]{3,2,1,0:T(8,128)(2,1)} %bitcast.53), calls=%async_computation.1 | async-start | bytes 9437184 | tf_op jit(solution)/shard_map/all_to_all | solution.py:247
  238.2 2.7 copy-start.5
  238.2 2.7 copy-start.7
  238.2 2.8 copy-start.9
  239.4 4.1 %copy-start.11 = (bf16[48,48,128]{2,0,1:T(8,128)(2,1)S(1)}, bf16[48,48,128]{2,0,1:T(8,128)(2,1)}, u32[]{:S(2)}) copy-start(bf16[48,48,128]{2,0,1:T(8,128)(2,1)} %copy-done.10) | copy-start | bytes 1769476
  239.6 4.0 %copy-start.3 = (bf16[128,128]{1,0:T(8,128)(2,1)S(1)}, bf16[128,128]{1,0:T(8,128)(2,1)}, u32[]{:S(2)}) copy-start(bf16[128,128]{1,0:T(8,128)(2,1)} %w_ref.2) | copy-start | bytes 98308
  251.6 2.2 copy-start
  253.8 2.2 copy-start.2

commit v4 on v3

--- a/solution.py
+++ b/solution.py
@@ -75,7 +75,8 @@
 
 
 def cross_kernel(b_ref, a_ref, o_ref):
-    nb, col_count, kg, rows, _ = o_ref.shape
+    nb, col_count, parts, kg, group, _ = o_ref.shape
+    rows = parts * group
     b = plane_rows(b_ref, 0, nb)
     step = kg * 128 // rows
     for c in range(col_count):
@@ -83,7 +84,7 @@
         res = lax.dot_general(b, a, (((1,), (1,)), ((), ())), preferred_element_type=jnp.float32)
         res = res.astype(jnp.bfloat16)
         for t in range(kg):
-            o_ref[:, c, t] = res[:, t * 128 : (t + 1) * 128].reshape(nb, rows, 128)
+            o_ref[:, c, :, t] = res[:, t * 128 : (t + 1) * 128].reshape(nb, parts, group, 128)
 
 
 def cross(own, row_count, col_count):
@@ -100,14 +101,18 @@
             pl.BlockSpec((nb, kgs, parts, None, group, 128), lambda j: (j, 0, 0, 1, 0, 0)),
             pl.BlockSpec((row_count, kgs, parts, None, group, 128), lambda j: (0, 0, 0, 0, 0, 0)),
         ],
-        out_specs=pl.BlockSpec((nb, col_count, kg, rows, 128), lambda j: (j, 0, 0, 0, 0)),
-        out_shape=jax.ShapeDtypeStruct((row_count, col_count, kg, rows, 128), jnp.bfloat16),
+        out_specs=pl.BlockSpec(
+            (nb, col_count, parts, kg, group, 128), lambda j: (j, 0, 0, 0, 0, 0)
+        ),
+        out_shape=jax.ShapeDtypeStruct(
+            (row_count, col_count, parts, kg, group, 128), jnp.bfloat16
+        ),
         compiler_params=params(56),
         cost_estimate=pl.CostEstimate(
             flops=2 * tokens**3, bytes_accessed=6 * tokens * tokens, transcendentals=0
         ),
         name="cross",
-    )(own, own).reshape(row_count * col_count, kg, rows, 128)
+    )(own, own).reshape(row_count * col_count, parts, kg, group, 128)
 
 
 def gate_kernel(z_ref, w_ref, g_ref):
@@ -144,48 +149,50 @@
 
 
 def finish_kernel(r_ref, z_ref, g_ref, w_ref, o_ref, scr):
-    hidden, jb, _ = r_ref.shape
+    hidden, groups, jb, _ = r_ref.shape
     width = w_ref.shape[1]
     batch = 4
-    scr[...] = r_ref[...].astype(jnp.float32).reshape(hidden * jb, 128)
-    for first in range(0, jb, batch):
-        parts = []
-        for j in range(first, first + batch):
-            v = scr[pl.ds(j, hidden, stride=jb), :]
-            mean = jnp.mean(v, axis=0, keepdims=True)
-            v = v - mean
-            var = jnp.mean(v * v, axis=0, keepdims=True)
-            parts.append((v * lax.rsqrt(var + 1e-5)).astype(jnp.bfloat16))
-        update = lax.dot_general(
-            jnp.concatenate(parts, axis=1),
-            w_ref[...],
-            (((0,), (0,)), ((), ())),
-            preferred_element_type=jnp.float32,
-        ).reshape(batch, 128, width)
-        at = pl.ds(first, batch)
-        o_ref[at] = (z_ref[at].astype(jnp.float32) + g_ref[at].astype(jnp.float32) * update).astype(jnp.bfloat16)
+    for t in range(groups):
+        scr[...] = r_ref[:, t].astype(jnp.float32).reshape(hidden * jb, 128)
+        for first in range(0, jb, batch):
+            parts = []
+            for j in range(first, first + batch):
+                v = scr[pl.ds(j, hidden, stride=jb), :]
+                mean = jnp.mean(v, axis=0, keepdims=True)
+                v = v - mean
+                var = jnp.mean(v * v, axis=0, keepdims=True)
+                parts.append((v * lax.rsqrt(var + 1e-5)).astype(jnp.bfloat16))
+            update = lax.dot_general(
+                jnp.concatenate(parts, axis=1),
+                w_ref[...],
+                (((0,), (0,)), ((), ())),
+                preferred_element_type=jnp.float32,
+            ).reshape(batch, 128, width)
+            at = (pl.ds(first, batch), pl.ds(t * 128, 128))
+            res = z_ref[at].astype(jnp.float32) + g_ref[at].astype(jnp.float32) * update
+            o_ref[at] = res.astype(jnp.bfloat16)
 
 
 def finish(returned, z, gate, w_out):
-    hidden, groups, rows, _ = returned.shape
-    _, cols, width = z.shape
-    tok = pl.BlockSpec((GB, 128, width), lambda j, t: (j, t, 0))
+    hidden, parts, groups, jb, _ = returned.shape
+    rows, cols, width = z.shape
+    tok = pl.BlockSpec((jb, cols, width), lambda j: (j, 0, 0))
     return pl.pallas_call(
         finish_kernel,
-        grid=(rows // GB, groups),
+        grid=(parts,),
         in_specs=[
-            pl.BlockSpec((hidden, None, GB, 128), lambda j, t: (0, t, j, 0)),
+            pl.BlockSpec((hidden, None, groups, jb, 128), lambda j: (0, j, 0, 0, 0)),
             tok,
             tok,
-            pl.BlockSpec((hidden, width), lambda j, t: (0, 0)),
+            pl.BlockSpec((hidden, width), lambda j: (0, 0)),
         ],
         out_specs=tok,
         out_shape=jax.ShapeDtypeStruct((rows, cols, width), jnp.bfloat16),
-        scratch_shapes=[pltpu.VMEM((hidden * GB, 128), jnp.float32)],
+        scratch_shapes=[pltpu.VMEM((hidden * jb, 128), jnp.float32)],
         compiler_params=params(56),
         cost_estimate=pl.CostEstimate(
             flops=2 * rows * cols * width * hidden,
-            bytes_accessed=10 * rows * cols * width,
+            bytes_accessed=8 * rows * cols * width,
             transcendentals=0,
         ),
         name="finish",
@@ -268,13 +275,15 @@
         return send(piece, low, high, onward, near)
 
     half0, half1 = first_leg(0, p[0]), first_leg(1, p[1])
-    got = {s: direct(s, p[s]) for s in (2, 3, 4)}
-    half0, half1, p0, p1, p5, p6, p7 = lax.optimization_barrier((half0, half1, p[0], p[1], p[5], p[6], p[7]))
+    got = {s: direct(s, p[s]) for s in (2, 3)}
+    in0 = inner(0, p[0])
+    half0, half1, rest = lax.optimization_barrier((half0, half1, [p[s] for s in (1, 4, 5, 6, 7)]))
     leg = second_leg(jnp.concatenate([half0, half1], axis=0))
-    got[5], got[6] = direct(5, p5), direct(6, p6)
-    in0, in1 = inner(0, p0), inner(1, p1)
+    for s in (4, 5, 6):
+        got[s] = direct(s, rest[s - 3])
+    in1 = inner(1, rest[0])
     got, leg, in0, in1, p7, both = lax.optimization_barrier(
-        (got, leg, in0, in1, p7, project(pair, w_in))
+        (got, leg, in0, in1, rest[4], project(pair, w_in))
     )
     own = exchange(both)
     own, p7 = lax.optimization_barrier((own, p7))

time: 310 us -> 305 us (0.984)
    dynamic_slice x7 -> x5, local copies, waits for them, and re-layouts: 6.6 us -> 4.62 us  [cut(): lax.dynamic_index_in_dim(pieces, lax.bitwise_xor(me, s), 1, keepdims=False)]
    unnamed x29 -> x25, local copies, waits for them, and re-layouts: 8.57 us -> 7.77 us
  transfers between devices with their start and end apart: 12 -> 12, of which waited for: 6 -> 5; matrix products, arithmetic and copies ran while one was open for 3% -> 3% of each run, Pallas kernels for 11% -> 12%
where the time goes in v4:
time: 305 us
  blocking collectives  116 us (38%)
  waiting for transfers between devices  81.8 us (27%)
  Pallas kernels  46.6 us (15%)
  starting transfers between devices  38.1 us (12%)
  local copies, waits for them, and re-layouts  20 us (7%)
    all_to_all x1, blocking collectives, exchange(): return lax.all_to_all(x, ALL, split_axis=0, concat_axis=0, tiled=True)  116 us
    ppermute x11, waiting for transfers between devices, send(): return lax.ppermute(piece, ALL, perm)  42.5 us
    all_to_all x1, waiting for transfers between devices, exchange(): return lax.all_to_all(x, ALL, split_axis=0, concat_axis=0, tiled=True)  39.3 us
    ppermute x11, starting transfers between devices, send(): return lax.ppermute(piece, ALL, perm)  31.1 us
    pallas_call x1, Pallas kernels, cross(): pl.pallas_call(cross_kernel, grid=(row_count // nb,), in_specs=[pl.BlockS...  14.2 us
    pallas_call x1, Pallas kernels, project(): pl.pallas_call(project_kernel, grid=(kg, rows // GB), in_specs=[pl.BlockS...  12.9 us
    pallas_call x1, Pallas kernels, finish(): pl.pallas_call(finish_kernel, grid=(parts,), in_specs=[pl.BlockSpec((hidd...  11.5 us
    pallas_call x1, Pallas kernels, gate_of(): pl.pallas_call(gate_kernel, grid=(rows // jb,), in_specs=[pl.BlockSpec((j...  8.03 us
  transfers between devices with their start and end apart: 12, of which 5 were waited for; matrix products, arithmetic and copies ran while one was open for 3% of the time, Pallas kernels for 12%

profile of v4, /device:TPU:1, one launch (start us, length us, event | category | flops | bytes accessed | tf_op | source)
XLA Modules:
  0.0 304.8 jit_solution(12456022529502168919)
XLA Ops:
  0.0 3.2 %constant_dynamic-slice_fusion = (bf16[48,1,48,128]{3,2,1,0:T(8,128)(2,1)S(1)}, bf16[48,1,48,128]{3,2,1,0:T(8,128)(2,1)S(1)}, bf16[48,1,48,128]{3,2,1,0:T(8,128)...) fusion(bf16[48,8,48,128]{3,2,1,0:T(8,128)(2,1)} %bitcast.47, ...), kind=kLoop, calls=%fused_computation.17 | loop fusion | bytes 9437216 | tf_op jit(solution)/shard_map/jit(dynamic_index_in_dim)/dynamic_slice | solution.py:207
  3.2 0.2 copy.24
  3.4 1.3 collective-permute-start.2
  4.7 1.0 copy.23
  5.6 1.3 collective-permute-start.3
  6.9 4.6 %collective-permute-start.8 = (bf16[48,48,128]{2,0,1:T(8,128)(2,1)S(1)}, bf16[48,48,128]{2,0,1:T(8,128)(2,1)S(1)}, u32[]{:S(2)}, u32[]{:S(2)}) collective-permute-start(bf16[48,48,128]{2,0,1:T(8,128)(2,1)S(1)} %bitcast.53), channel_id=1, source_target_pairs={{0,0},{1,32},{4,4},{5,36},{8,8},{9,40},{12,12},{13,44},{16,16},{17... | collective-permute-start | bytes 1769480 | tf_op jit(solution)/shard_map/ppermute | solution.py:220
  11.5 0.0 copy-start.11
  11.5 0.2 copy.26
  11.7 1.4 collective-permute-start
  13.1 0.2 copy.25
  13.3 2.3 collective-permute-start.1
  15.6 1.4 copy_bitcast_fusion
  17.0 1.4 copy_bitcast_fusion.2
  18.4 16.9 %collective-permute-done.2 = bf16[48,48,128]{2,0,1:T(8,128)(2,1)S(1)} collective-permute-done((bf16[48,48,128]{2,0,1:T(8,128)(2,1)S(1)}, bf16[48,48,128]{2,0,1:T(8,128)(2,1)S(1)}, u32[]{:S(2)}, u32[]{:S(2)}) %collective-permute-start.2) | collective-permute-done | bytes 589856 | tf_op jit(solution)/shard_map/ppermute | solution.py:220
  35.3 0.0 collective-permute-done.3
  35.3 0.1 pad_maximum_fusion
  35.4 4.3 %collective-permute-start.7 = (bf16[96,48,128]{2,0,1:T(8,128)(2,1)S(1)}, bf16[96,48,128]{2,0,1:T(8,128)(2,1)S(1)}, u32[]{:S(2)}, u32[]{:S(2)}) collective-permute-start(bf16[96,48,128]{2,0,1:T(8,128)(2,1)S(1)} %pad_maximum_fusion), channel_id=1, source_target_pairs={{0,2},{1,3},{4,6},{5,7},{8,10},{9,11},{12,14},{13,15},{16,18},{17,... | collective-permute-start | bytes 3538952 | tf_op jit(solution)/shard_map/ppermute | solution.py:220
  39.7 4.1 %collective-permute-start.4 = (bf16[48,48,128]{2,0,1:T(8,128)(2,1)}, bf16[48,48,128]{2,0,1:T(8,128)(2,1)}, u32[]{:S(2)}, u32[]{:S(2)}) collective-permute-start(bf16[48,48,128]{2,0,1:T(8,128)(2,1)} %get-tuple-element.26), channel_id=1, source_target_pairs={{0,16},{1,48},{2,80},{3,112},{4,20},{5,52},{6,84},{7,116},{8,24},{... | collective-permute-start | bytes 1769480 | tf_op jit(solution)/shard_map/ppermute | solution.py:220
  43.8 0.0 collective-permute-done
  43.8 5.1 %collective-permute-start.5 = (bf16[48,48,128]{2,0,1:T(8,128)(2,1)}, bf16[48,48,128]{2,0,1:T(8,128)(2,1)}, u32[]{:S(2)}, u32[]{:S(2)}) collective-permute-start(bf16[48,48,128]{2,0,1:T(8,128)(2,1)} %get-tuple-element.27), channel_id=1, source_target_pairs={{0,20},{1,52},{2,84},{3,116},{4,16},{5,48},{6,80},{7,112},{8,28},{... | collective-permute-start | bytes 1769480 | tf_op jit(solution)/shard_map/ppermute | solution.py:220
  48.9 0.0 collective-permute-done.1
  48.9 3.6 %collective-permute-start.6 = (bf16[48,48,128]{2,0,1:T(8,128)(2,1)}, bf16[48,48,128]{2,0,1:T(8,128)(2,1)}, u32[]{:S(2)}, u32[]{:S(2)}) collective-permute-start(bf16[48,48,128]{2,0,1:T(8,128)(2,1)} %get-tuple-element.28), channel_id=1, source_target_pairs={{0,24},{1,56},{2,88},{3,120},{4,28},{5,60},{6,92},{7,124},{8,16},{... | collective-permute-start | bytes 1769480 | tf_op jit(solution)/shard_map/ppermute | solution.py:220
  52.5 0.0 collective-permute-done.8
  52.5 0.0 copy-done.4
  52.5 0.0 copy-done.6
  52.5 1.9 collective-permute-start.9
  54.4 0.0 copy-done.11
  54.4 0.1 copy.13
  54.6 0.0 copy-start.1
  54.6 2.3 copy-done.1
  56.9 12.9 %project.1 = bf16[128,3,3,2,16,128]{5,4,3,2,1,0:T(8,128)(2,1)S(1)} custom-call(bf16[48,384,128]{2,1,0:T(8,128)(2,1)S(1)} %copy-done.1, bf16[512,128]{1,0:T(8,128)(2,1)S(1)} %bitcast.48), custom_call_target="tpu_custom_call" | custom-call | flops 2415919104 | bytes 14155776 | tf_op jit(solution)/shard_map/project/pallas_call | solution.py:49
  69.8 0.0 copy-start.10
  69.8 0.0 collective-permute-done.4
  69.8 14.2 %collective-permute-done.5 = bf16[48,48,128]{2,0,1:T(8,128)(2,1)} collective-permute-done((bf16[48,48,128]{2,0,1:T(8,128)(2,1)}, bf16[48,48,128]{2,0,1:T(8,128)(2,1)}, u32[]{:S(2)}, u32[]{:S(2)}) %collective-permute-start.5) | collective-permute-done | bytes 589856 | tf_op jit(solution)/shard_map/ppermute | solution.py:220
  84.0 0.0 collective-permute-done.6
  84.0 8.3 %collective-permute-done.9 = bf16[48,48,128]{2,0,1:T(8,128)(2,1)} collective-permute-done((bf16[48,48,128]{2,0,1:T(8,128)(2,1)}, bf16[48,48,128]{2,0,1:T(8,128)(2,1)}, u32[]{:S(2)}, u32[]{:S(2)}) %collective-permute-start.9) | collective-permute-done | bytes 589856 | tf_op jit(solution)/shard_map/ppermute | solution.py:220
  92.3 0.0 collective-permute-done.7
  92.3 116.5 %all_to_all.10 = bf16[128,3,3,2,16,128]{5,4,3,2,1,0:T(8,128)(2,1)} all-to-all(bf16[128,3,3,2,16,128]{5,4,3,2,1,0:T(8,128)(2,1)S(1)} %project.1), channel_id=1, replica_groups=mesh['row'=32,'col'=4] {'row','col'}, dimensions={0} | all-to-all | bytes 18874368 | tf_op jit(solution)/shard_map/all_to_all | solution.py:254
  208.8 0.0 copy-done.10
  208.8 1.3 collective-permute-start.10
  210.0 14.2 %cross.1 = bf16[32,4,3,3,16,128]{5,4,3,2,1,0:T(8,128)(2,1)} custom-call(bf16[32,12,3,2,16,128]{5,4,3,2,1,0:T(8,128)(2,1)} %bitcast.49, bf16[32,12,3,2,16,128]{5,4,3,2,1,0:T(8,128)(2,1)} %bitcast.50), custom_call_target="tpu_custom_call" | custom-call | flops 7247757312 | bytes 14155776 | tf_op jit(solution)/shard_map/cross/pallas_call | solution.py:97
  224.2 3.0 collective-permute-done.10
  227.3 0.9 copy-done.8
  228.1 6.9 %all-to-all-start.1 = ((bf16[128,3,3,16,128]{4,3,2,1,0:T(8,128)(2,1)}), bf16[128,3,3,16,128]{4,3,2,1,0:T(8,128)(2,1)}, u32[]{:S(2)}, u32[]{:S(2)}) async-start(bf16[128,3,3,16,128]{4,3,2,1,0:T(8,128)(2,1)} %bitcast.51), calls=%async_computation.1 | async-start | bytes 9437184 | tf_op jit(solution)/shard_map/all_to_all | solution.py:254
  235.1 0.0 copy-start.5
  235.1 0.0 copy-start.7
  235.1 1.1 broadcast_in_dim.28
  236.3 0.0 copy-start.9
  236.3 0.2 bitcast_dynamic-update-slice_fusion
  236.5 0.0 copy-start.3
  236.5 1.3 bitcast_dynamic-update-slice_fusion.7
  237.8 0.0 copy-done.5
  237.8 0.1 bitcast_dynamic-update-slice_fusion.6
  237.9 0.0 copy-done.7
  237.9 0.1 bitcast_dynamic-update-slice_fusion.5
  238.0 1.1 bitcast_dynamic-update-slice_fusion.4
  239.1 1.1 bitcast_dynamic-update-slice_fusion.3
  240.3 1.1 bitcast_dynamic-update-slice_fusion.2
  241.4 0.1 bitcast_dynamic-update-slice_fusion.1
  241.5 8.0 %gate.1.g_ref = bf16[48,384,128]{2,1,0:T(8,128)(2,1)S(1)} custom-call(bf16[48,384,128]{2,1,0:T(8,128)(2,1)S(1)} %bitcast.45, bf16[128,128]{1,0:T(8,128)(2,1)S(1)} %copy-done.3), custom_call_target="tpu_custom_call" | custom-call | flops 603979776 | bytes 14155776 | tf_op jit(solution)/shard_map/gate/pallas_call | solution.py:132
  249.6 2.2 copy-done
  251.8 2.2 copy-done.2
  254.0 39.3 %all-to-all-done.1.r_ref = bf16[128,3,3,16,128]{4,3,2,1,0:T(8,128)(2,1)} async-done(((bf16[128,3,3,16,128]{4,3,2,1,0:T(8,128)(2,1)}), bf16[128,3,3,16,128]{4,3,2,1,0:T(8,128)(2,1)}, u32[]{:S(2)}, u32[]{:S(2)}) %all-to-all-start.1) | async-done | bytes 4718624 | tf_op jit(solution)/shard_map/all_to_all | solution.py:254
  293.3 11.5 %finish.1 = bf16[48,384,128]{2,1,0:T(8,128)(2,1)} custom-call(bf16[128,3,3,16,128]{4,3,2,1,0:T(8,128)(2,1)} %all-to-all-done.1.r_ref, bf16[48,384,128]{2,1,0:T(8,128)(2,1)} %bitcast.46, bf16[48,384,128]{2,1,0:T(8,128)(2,1)} %copy-done.2, bf16[128,128]{1,0:T(8,128)(2,1)} %w_ref.3), custom_call_target="tpu_custom_call" | custom-call | flops 603979776 | bytes 18874368 | tf_op jit(solution)/shard_map/finish/pallas_call | solution.py:180
  (7 shorter events, 0.0 us)
Async XLA Ops:
  3.4 31.9 %collective-permute-start.2 = (bf16[48,48,128]{2,0,1:T(8,128)(2,1)S(1)}, bf16[48,48,128]{2,0,1:T(8,128)(2,1)S(1)}, u32[]{:S(2)}, u32[]{:S(2)}) collective-permute-start(bf16[48,48,128]{2,0,1:T(8,128)(2,1)S(1)} %bitcast.52), channel_id=1, source_target_pairs={{2,66},{3,98},{6,70},{7,102},{10,74},{11,106},{14,78},{15,110},{18... | collective-permute-start | bytes 1769480 | tf_op jit(solution)/shard_map/ppermute | solution.py:220
  5.6 29.7 %collective-permute-start.3 = (bf16[48,48,128]{2,0,1:T(8,128)(2,1)}, bf16[48,48,128]{2,0,1:T(8,128)(2,1)S(1)}, u32[]{:S(2)}, u32[]{:S(2)}) collective-permute-start(bf16[48,48,128]{2,0,1:T(8,128)(2,1)} %bitcast.41), channel_id=1, source_target_pairs={{2,70},{3,102},{6,66},{7,98},{10,78},{11,110},{14,74},{15,106},{18... | collective-permute-start | bytes 1769480 | tf_op jit(solution)/shard_map/ppermute | solution.py:220
  6.9 45.6 %collective-permute-start.8 = (bf16[48,48,128]{2,0,1:T(8,128)(2,1)S(1)}, bf16[48,48,128]{2,0,1:T(8,128)(2,1)S(1)}, u32[]{:S(2)}, u32[]{:S(2)}) collective-permute-start(bf16[48,48,128]{2,0,1:T(8,128)(2,1)S(1)} %bitcast.53), channel_id=1, source_target_pairs={{0,0},{1,32},{4,4},{5,36},{8,8},{9,40},{12,12},{13,44},{16,16},{17... | collective-permute-start | bytes 1769480 | tf_op jit(solution)/shard_map/ppermute | solution.py:220
  11.5 42.9 %copy-start.11 = (bf16[128,512]{1,0:T(8,128)(2,1)S(1)}, bf16[128,512]{1,0:T(8,128)(2,1)}, u32[]{:S(2)}) copy-start(bf16[128,512]{1,0:T(8,128)(2,1)} %param.5) | copy-start | bytes 393220
  11.7 32.1 %collective-permute-start = (bf16[48,48,128]{2,0,1:T(8,128)(2,1)S(1)}, bf16[48,48,128]{2,0,1:T(8,128)(2,1)S(1)}, u32[]{:S(2)}, u32[]{:S(2)}) collective-permute-start(bf16[48,48,128]{2,0,1:T(8,128)(2,1)S(1)} %bitcast.55), channel_id=1, source_target_pairs={{0,8},{1,40},{2,72},{3,104},{4,12},{5,44},{6,76},{7,108},{8,0},{9,... | collective-permute-start | bytes 1769480 | tf_op jit(solution)/shard_map/ppermute | solution.py:220
  13.3 35.6 %collective-permute-start.1 = (bf16[48,48,128]{2,0,1:T(8,128)(2,1)S(1)}, bf16[48,48,128]{2,0,1:T(8,128)(2,1)S(1)}, u32[]{:S(2)}, u32[]{:S(2)}) collective-permute-start(bf16[48,48,128]{2,0,1:T(8,128)(2,1)S(1)} %bitcast.54), channel_id=1, source_target_pairs={{0,12},{1,44},{2,76},{3,108},{4,8},{5,40},{6,72},{7,104},{8,4},{9,... | collective-permute-start | bytes 1769480 | tf_op jit(solution)/shard_map/ppermute | solution.py:220
  35.4 56.9 %collective-permute-start.7 = (bf16[96,48,128]{2,0,1:T(8,128)(2,1)S(1)}, bf16[96,48,128]{2,0,1:T(8,128)(2,1)S(1)}, u32[]{:S(2)}, u32[]{:S(2)}) collective-permute-start(bf16[96,48,128]{2,0,1:T(8,128)(2,1)S(1)} %pad_maximum_fusion), channel_id=1, source_target_pairs={{0,2},{1,3},{4,6},{5,7},{8,10},{9,11},{12,14},{13,15},{16,18},{17,... | collective-permute-start | bytes 3538952 | tf_op jit(solution)/shard_map/ppermute | solution.py:220
  39.7 30.0 %collective-permute-start.4 = (bf16[48,48,128]{2,0,1:T(8,128)(2,1)}, bf16[48,48,128]{2,0,1:T(8,128)(2,1)}, u32[]{:S(2)}, u32[]{:S(2)}) collective-permute-start(bf16[48,48,128]{2,0,1:T(8,128)(2,1)} %get-tuple-element.26), channel_id=1, source_target_pairs={{0,16},{1,48},{2,80},{3,112},{4,20},{5,52},{6,84},{7,116},{8,24},{... | collective-permute-start | bytes 1769480 | tf_op jit(solution)/shard_map/ppermute | solution.py:220
  43.8 8.7 %copy-start.4 = (bf16[48,48,128]{2,0,1:T(8,128)(2,1)}, bf16[48,48,128]{2,0,1:T(8,128)(2,1)S(1)}, u32[]{:S(2)}) copy-start(bf16[48,48,128]{2,0,1:T(8,128)(2,1)S(1)} %collective-permute-done) | copy-start | bytes 1769476
  43.8 40.2 %collective-permute-start.5 = (bf16[48,48,128]{2,0,1:T(8,128)(2,1)}, bf16[48,48,128]{2,0,1:T(8,128)(2,1)}, u32[]{:S(2)}, u32[]{:S(2)}) collective-permute-start(bf16[48,48,128]{2,0,1:T(8,128)(2,1)} %get-tuple-element.27), channel_id=1, source_target_pairs={{0,20},{1,52},{2,84},{3,116},{4,16},{5,48},{6,80},{7,112},{8,28},{... | collective-permute-start | bytes 1769480 | tf_op jit(solution)/shard_map/ppermute | solution.py:220
  48.9 3.6 %copy-start.6 = (bf16[48,48,128]{2,0,1:T(8,128)(2,1)}, bf16[48,48,128]{2,0,1:T(8,128)(2,1)S(1)}, u32[]{:S(2)}) copy-start(bf16[48,48,128]{2,0,1:T(8,128)(2,1)S(1)} %collective-permute-done.1) | copy-start | bytes 1769476
  48.9 35.1 %collective-permute-start.6 = (bf16[48,48,128]{2,0,1:T(8,128)(2,1)}, bf16[48,48,128]{2,0,1:T(8,128)(2,1)}, u32[]{:S(2)}, u32[]{:S(2)}) collective-permute-start(bf16[48,48,128]{2,0,1:T(8,128)(2,1)} %get-tuple-element.28), channel_id=1, source_target_pairs={{0,24},{1,56},{2,88},{3,120},{4,28},{5,60},{6,92},{7,124},{8,16},{... | collective-permute-start | bytes 1769480 | tf_op jit(solution)/shard_map/ppermute | solution.py:220
  52.5 39.8 %collective-permute-start.9 = (bf16[48,48,128]{2,0,1:T(8,128)(2,1)}, bf16[48,48,128]{2,0,1:T(8,128)(2,1)}, u32[]{:S(2)}, u32[]{:S(2)}) collective-permute-start(bf16[48,48,128]{2,0,1:T(8,128)(2,1)} %bitcast.41), channel_id=1, source_target_pairs={{0,4},{1,36},{4,0},{5,32},{8,12},{9,44},{12,8},{13,40},{16,20},{17... | collective-permute-start | bytes 1769480 | tf_op jit(solution)/shard_map/ppermute | solution.py:220
  54.6 2.3 copy-start.1
  69.8 139.0 %copy-start.10 = (bf16[48,48,128]{2,0,1:T(8,128)(2,1)S(1)}, bf16[48,48,128]{2,0,1:T(8,128)(2,1)}, u32[]{:S(2)}) copy-start(bf16[48,48,128]{2,0,1:T(8,128)(2,1)} %get-tuple-element.35) | copy-start | bytes 1769476
  208.8 18.5 %collective-permute-start.10 = (bf16[48,48,128]{2,0,1:T(8,128)(2,1)S(1)}, bf16[48,48,128]{2,0,1:T(8,128)(2,1)S(1)}, u32[]{:S(2)}, u32[]{:S(2)}) collective-permute-start(bf16[48,48,128]{2,0,1:T(8,128)(2,1)S(1)} %copy-done.10), channel_id=1, source_target_pairs={{0,28},{1,60},{2,92},{3,124},{4,24},{5,56},{6,88},{7,120},{8,20},{... | collective-permute-start | bytes 1769480 | tf_op jit(solution)/shard_map/ppermute | solution.py:220
  227.3 0.9 copy-start.8
  228.1 65.2 %all-to-all-start.1 = ((bf16[128,3,3,16,128]{4,3,2,1,0:T(8,128)(2,1)}), bf16[128,3,3,16,128]{4,3,2,1,0:T(8,128)(2,1)}, u32[]{:S(2)}, u32[]{:S(2)}) async-start(bf16[128,3,3,16,128]{4,3,2,1,0:T(8,128)(2,1)} %bitcast.51), calls=%async_computation.1 | async-start | bytes 9437184 | tf_op jit(solution)/shard_map/all_to_all | solution.py:254
  235.1 2.7 copy-start.5
  235.1 2.7 copy-start.7
  236.3 5.2 %copy-start.9 = (bf16[48,48,128]{2,0,1:T(8,128)(2,1)S(1)}, bf16[48,48,128]{2,0,1:T(8,128)(2,1)}, u32[]{:S(2)}) copy-start(bf16[48,48,128]{2,0,1:T(8,128)(2,1)} %copy-done.8) | copy-start | bytes 1769476
  236.5 5.0 %copy-start.3 = (bf16[128,128]{1,0:T(8,128)(2,1)S(1)}, bf16[128,128]{1,0:T(8,128)(2,1)}, u32[]{:S(2)}) copy-start(bf16[128,128]{1,0:T(8,128)(2,1)} %w_ref.2) | copy-start | bytes 98308
  249.6 2.2 copy-start
  251.8 2.2 copy-start.2

commit v5 on v4

--- a/solution.py
+++ b/solution.py
@@ -7,6 +7,7 @@
 
 ALL = ("row", "col")
 GB = 16
+PITCH = 24
 
 
 def sigmoid(x):
@@ -53,8 +54,8 @@
             pl.BlockSpec((GB, 128, width), lambda k, i: (i, k, 0)),
             pl.BlockSpec((4 * hidden, width), lambda k, i: (0, 0)),
         ],
-        out_specs=pl.BlockSpec((hidden, None, None, 2, GB, 128), lambda k, i: (0, k, i, 0, 0, 0)),
-        out_shape=jax.ShapeDtypeStruct((hidden, kg, rows // GB, 2, GB, 128), jnp.bfloat16),
+        out_specs=pl.BlockSpec((hidden, None, 2, GB, 128), lambda k, i: (0, k, 0, i, 0)),
+        out_shape=jax.ShapeDtypeStruct((hidden, kg, 2, rows, 128), jnp.bfloat16),
         scratch_shapes=[pltpu.VMEM((hidden * GB, 128), jnp.float32)] * 2,
         compiler_params=params(16),
         cost_estimate=pl.CostEstimate(
@@ -66,43 +67,40 @@
     )(pair, w_in.T)
 
 
-def plane_rows(ref, first, count):
-    _, kgs, parts, group, lanes = ref.shape
-    return jnp.concatenate(
-        [ref[pl.ds(first, count), q].reshape(count * parts * group, lanes) for q in range(kgs)],
-        axis=1,
-    )
+def plane_rows(ref):
+    count, kgs, rows, lanes = ref.shape
+    return jnp.concatenate([ref[:, q].reshape(count * rows, lanes) for q in range(kgs)], axis=1)
 
 
 def cross_kernel(b_ref, a_ref, o_ref):
-    nb, col_count, parts, kg, group, _ = o_ref.shape
-    rows = parts * group
-    b = plane_rows(b_ref, 0, nb)
-    step = kg * 128 // rows
-    for c in range(col_count):
-        a = plane_rows(a_ref, c * step, step)
-        res = lax.dot_general(b, a, (((1,), (1,)), ((), ())), preferred_element_type=jnp.float32)
-        res = res.astype(jnp.bfloat16)
-        for t in range(kg):
-            o_ref[:, c, :, t] = res[:, t * 128 : (t + 1) * 128].reshape(nb, parts, group, 128)
+    row_count, parts, kg, group, _ = o_ref.shape
+    res = lax.dot_general(
+        plane_rows(b_ref),
+        plane_rows(a_ref),
+        (((1,), (1,)), ((), ())),
+        preferred_element_type=jnp.float32,
+    ).astype(jnp.bfloat16)
+    for t in range(kg):
+        o_ref[:, :, t] = res[:, t * 128 : (t + 1) * 128].reshape(row_count, parts, group, 128)
 
 
 def cross(own, row_count, col_count):
-    _, kg, parts, _, group, _ = own.shape
-    rows = parts * group
+    _, kg, _, rows, _ = own.shape
+    group = GB
+    parts = rows // group
     kgs = col_count * kg
-    own = own.reshape(row_count, kgs, parts, 2, group, 128)
-    nb = 8
+    own = own.reshape(row_count, kgs, 2, rows, 128)
+    low = row_count // col_count
     tokens = row_count * rows
     return pl.pallas_call(
         cross_kernel,
-        grid=(row_count // nb,),
+        grid=(col_count,),
         in_specs=[
-            pl.BlockSpec((nb, kgs, parts, None, group, 128), lambda j: (j, 0, 0, 1, 0, 0)),
-            pl.BlockSpec((row_count, kgs, parts, None, group, 128), lambda j: (0, 0, 0, 0, 0, 0)),
+            pl.BlockSpec((row_count, kgs, None, rows, 128), lambda c: (0, 0, 1, 0, 0)),
+            pl.BlockSpec((low, kgs, None, rows, 128), lambda c: (c, 0, 0, 0, 0)),
         ],
         out_specs=pl.BlockSpec(
-            (nb, col_count, parts, kg, group, 128), lambda j: (j, 0, 0, 0, 0, 0)
+            (row_count, None, parts, kg, group, 128), lambda c: (0, c, 0, 0, 0, 0)
         ),
         out_shape=jax.ShapeDtypeStruct(
             (row_count, col_count, parts, kg, group, 128), jnp.bfloat16
@@ -153,15 +151,15 @@
     width = w_ref.shape[1]
     batch = 4
     for t in range(groups):
-        scr[...] = r_ref[:, t].astype(jnp.float32).reshape(hidden * jb, 128)
+        v = r_ref[:, t].astype(jnp.float32)
+        v = v - jnp.mean(v, axis=0, keepdims=True)
+        var = jnp.mean(v * v, axis=0, keepdims=True)
+        scr.reshape(hidden, PITCH, 128)[:, :jb, :] = v * lax.rsqrt(var + 1e-5)
         for first in range(0, jb, batch):
-            parts = []
-            for j in range(first, first + batch):
-                v = scr[pl.ds(j, hidden, stride=jb), :]
-                mean = jnp.mean(v, axis=0, keepdims=True)
-                v = v - mean
-                var = jnp.mean(v * v, axis=0, keepdims=True)
-                parts.append((v * lax.rsqrt(var + 1e-5)).astype(jnp.bfloat16))
+            parts = [
+                scr[pl.ds(j, hidden, stride=PITCH), :].astype(jnp.bfloat16)
+                for j in range(first, first + batch)
+            ]
             update = lax.dot_general(
                 jnp.concatenate(parts, axis=1),
                 w_ref[...],
@@ -188,7 +186,7 @@
         ],
         out_specs=tok,
         out_shape=jax.ShapeDtypeStruct((rows, cols, width), jnp.bfloat16),
-        scratch_shapes=[pltpu.VMEM((hidden * jb, 128), jnp.float32)],
+        scratch_shapes=[pltpu.VMEM((hidden * PITCH, 128), jnp.float32)],
         compiler_params=params(56),
         cost_estimate=pl.CostEstimate(
             flops=2 * rows * cols * width * hidden,

time: 305 us -> 304 us (level)
  no operation moved by 1% of the time
where the time goes in v5:
time: 304 us
  blocking collectives  116 us (38%)
  waiting for transfers between devices  81.6 us (27%)
  Pallas kernels  46 us (15%)
  starting transfers between devices  38.1 us (13%)
  local copies, waits for them, and re-layouts  20 us (7%)
    all_to_all x1, blocking collectives, exchange(): return lax.all_to_all(x, ALL, split_axis=0, concat_axis=0, tiled=True)  116 us
    ppermute x11, waiting for transfers between devices, send(): return lax.ppermute(piece, ALL, perm)  42.3 us
    all_to_all x1, waiting for transfers between devices, exchange(): return lax.all_to_all(x, ALL, split_axis=0, concat_axis=0, tiled=True)  39.3 us
    ppermute x11, starting transfers between devices, send(): return lax.ppermute(piece, ALL, perm)  31.1 us
    pallas_call x1, Pallas kernels, cross(): pl.pallas_call(cross_kernel, grid=(col_count,), in_specs=[pl.BlockSpec((r...  14.4 us
    pallas_call x1, Pallas kernels, project(): pl.pallas_call(project_kernel, grid=(kg, rows // GB), in_specs=[pl.BlockS...  12.9 us
    pallas_call x1, Pallas kernels, finish(): pl.pallas_call(finish_kernel, grid=(parts,), in_specs=[pl.BlockSpec((hidd...  10.7 us
    pallas_call x1, Pallas kernels, gate_of(): pl.pallas_call(gate_kernel, grid=(rows // jb,), in_specs=[pl.BlockSpec((j...  8.03 us
  transfers between devices with their start and end apart: 12, of which 5 were waited for; matrix products, arithmetic and copies ran while one was open for 3% of the time, Pallas kernels for 12%

profile of v5, /device:TPU:1, one launch (start us, length us, event | category | flops | bytes accessed | tf_op | source)
XLA Modules:
  0.0 304.0 jit_solution(7603317554507078288)
XLA Ops:
  0.0 3.2 %constant_dynamic-slice_fusion = (bf16[48,1,48,128]{3,2,1,0:T(8,128)(2,1)S(1)}, bf16[48,1,48,128]{3,2,1,0:T(8,128)(2,1)S(1)}, bf16[48,1,48,128]{3,2,1,0:T(8,128)...) fusion(bf16[48,8,48,128]{3,2,1,0:T(8,128)(2,1)} %bitcast.47, ...), kind=kLoop, calls=%fused_computation.17 | loop fusion | bytes 9437216 | tf_op jit(solution)/shard_map/jit(dynamic_index_in_dim)/dynamic_slice | solution.py:205
  3.2 0.2 copy.24
  3.4 1.3 collective-permute-start.2
  4.7 1.0 copy.23
  5.6 1.3 collective-permute-start.3
  6.9 4.6 %collective-permute-start.8 = (bf16[48,48,128]{2,0,1:T(8,128)(2,1)S(1)}, bf16[48,48,128]{2,0,1:T(8,128)(2,1)S(1)}, u32[]{:S(2)}, u32[]{:S(2)}) collective-permute-start(bf16[48,48,128]{2,0,1:T(8,128)(2,1)S(1)} %bitcast.53), channel_id=1, source_target_pairs={{0,0},{1,32},{4,4},{5,36},{8,8},{9,40},{12,12},{13,44},{16,16},{17... | collective-permute-start | bytes 1769480 | tf_op jit(solution)/shard_map/ppermute | solution.py:218
  11.5 0.0 copy-start.11
  11.5 0.2 copy.26
  11.7 1.4 collective-permute-start
  13.1 0.2 copy.25
  13.3 2.3 collective-permute-start.1
  15.6 1.4 copy_bitcast_fusion
  17.0 1.4 copy_bitcast_fusion.2
  18.4 16.9 %collective-permute-done.2 = bf16[48,48,128]{2,0,1:T(8,128)(2,1)S(1)} collective-permute-done((bf16[48,48,128]{2,0,1:T(8,128)(2,1)S(1)}, bf16[48,48,128]{2,0,1:T(8,128)(2,1)S(1)}, u32[]{:S(2)}, u32[]{:S(2)}) %collective-permute-start.2) | collective-permute-done | bytes 589856 | tf_op jit(solution)/shard_map/ppermute | solution.py:218
  35.3 0.0 collective-permute-done.3
  35.3 0.1 pad_maximum_fusion
  35.4 4.3 %collective-permute-start.7 = (bf16[96,48,128]{2,0,1:T(8,128)(2,1)S(1)}, bf16[96,48,128]{2,0,1:T(8,128)(2,1)S(1)}, u32[]{:S(2)}, u32[]{:S(2)}) collective-permute-start(bf16[96,48,128]{2,0,1:T(8,128)(2,1)S(1)} %pad_maximum_fusion), channel_id=1, source_target_pairs={{0,2},{1,3},{4,6},{5,7},{8,10},{9,11},{12,14},{13,15},{16,18},{17,... | collective-permute-start | bytes 3538952 | tf_op jit(solution)/shard_map/ppermute | solution.py:218
  39.7 4.1 %collective-permute-start.4 = (bf16[48,48,128]{2,0,1:T(8,128)(2,1)}, bf16[48,48,128]{2,0,1:T(8,128)(2,1)}, u32[]{:S(2)}, u32[]{:S(2)}) collective-permute-start(bf16[48,48,128]{2,0,1:T(8,128)(2,1)} %get-tuple-element.26), channel_id=1, source_target_pairs={{0,16},{1,48},{2,80},{3,112},{4,20},{5,52},{6,84},{7,116},{8,24},{... | collective-permute-start | bytes 1769480 | tf_op jit(solution)/shard_map/ppermute | solution.py:218
  43.8 0.0 collective-permute-done
  43.8 5.1 %collective-permute-start.5 = (bf16[48,48,128]{2,0,1:T(8,128)(2,1)}, bf16[48,48,128]{2,0,1:T(8,128)(2,1)}, u32[]{:S(2)}, u32[]{:S(2)}) collective-permute-start(bf16[48,48,128]{2,0,1:T(8,128)(2,1)} %get-tuple-element.27), channel_id=1, source_target_pairs={{0,20},{1,52},{2,84},{3,116},{4,16},{5,48},{6,80},{7,112},{8,28},{... | collective-permute-start | bytes 1769480 | tf_op jit(solution)/shard_map/ppermute | solution.py:218
  48.9 0.0 collective-permute-done.1
  48.9 3.6 %collective-permute-start.6 = (bf16[48,48,128]{2,0,1:T(8,128)(2,1)}, bf16[48,48,128]{2,0,1:T(8,128)(2,1)}, u32[]{:S(2)}, u32[]{:S(2)}) collective-permute-start(bf16[48,48,128]{2,0,1:T(8,128)(2,1)} %get-tuple-element.28), channel_id=1, source_target_pairs={{0,24},{1,56},{2,88},{3,120},{4,28},{5,60},{6,92},{7,124},{8,16},{... | collective-permute-start | bytes 1769480 | tf_op jit(solution)/shard_map/ppermute | solution.py:218
  52.5 0.0 collective-permute-done.8
  52.5 0.0 copy-done.4
  52.5 0.0 copy-done.6
  52.5 1.9 collective-permute-start.9
  54.4 0.0 copy-done.11
  54.4 0.1 copy.13
  54.6 0.0 copy-start.1
  54.6 2.3 copy-done.1
  56.9 12.9 %project.1 = bf16[128,3,2,48,128]{4,3,2,1,0:T(8,128)(2,1)S(1)} custom-call(bf16[48,384,128]{2,1,0:T(8,128)(2,1)S(1)} %copy-done.1, bf16[512,128]{1,0:T(8,128)(2,1)S(1)} %bitcast.48), custom_call_target="tpu_custom_call" | custom-call | flops 2415919104 | bytes 14155776 | tf_op jit(solution)/shard_map/project/pallas_call | solution.py:50
  69.8 0.0 copy-start.10
  69.8 0.0 collective-permute-done.4
  69.8 14.2 %collective-permute-done.5 = bf16[48,48,128]{2,0,1:T(8,128)(2,1)} collective-permute-done((bf16[48,48,128]{2,0,1:T(8,128)(2,1)}, bf16[48,48,128]{2,0,1:T(8,128)(2,1)}, u32[]{:S(2)}, u32[]{:S(2)}) %collective-permute-start.5) | collective-permute-done | bytes 589856 | tf_op jit(solution)/shard_map/ppermute | solution.py:218
  84.0 0.0 collective-permute-done.6
  84.0 8.3 %collective-permute-done.9 = bf16[48,48,128]{2,0,1:T(8,128)(2,1)} collective-permute-done((bf16[48,48,128]{2,0,1:T(8,128)(2,1)}, bf16[48,48,128]{2,0,1:T(8,128)(2,1)}, u32[]{:S(2)}, u32[]{:S(2)}) %collective-permute-start.9) | collective-permute-done | bytes 589856 | tf_op jit(solution)/shard_map/ppermute | solution.py:218
  92.3 0.0 collective-permute-done.7
  92.3 116.5 %all_to_all.10 = bf16[128,3,2,48,128]{4,3,2,1,0:T(8,128)(2,1)} all-to-all(bf16[128,3,2,48,128]{4,3,2,1,0:T(8,128)(2,1)S(1)} %project.1), channel_id=1, replica_groups=mesh['row'=32,'col'=4] {'row','col'}, dimensions={0} | all-to-all | bytes 18874368 | tf_op jit(solution)/shard_map/all_to_all | solution.py:252
  208.8 0.0 copy-done.10
  208.8 1.3 collective-permute-start.10
  210.0 14.4 %cross.1 = bf16[32,4,3,3,16,128]{5,4,3,2,1,0:T(8,128)(2,1)} custom-call(bf16[32,12,2,48,128]{4,3,2,1,0:T(8,128)(2,1)} %bitcast.49, bf16[32,12,2,48,128]{4,3,2,1,0:T(8,128)(2,1)} %bitcast.50), custom_call_target="tpu_custom_call" | custom-call | flops 7247757312 | bytes 14155776 | tf_op jit(solution)/shard_map/cross/pallas_call | solution.py:95
  224.4 2.8 collective-permute-done.10
  227.3 0.9 copy-done.8
  228.1 6.9 %all-to-all-start.1 = ((bf16[128,3,3,16,128]{4,3,2,1,0:T(8,128)(2,1)}), bf16[128,3,3,16,128]{4,3,2,1,0:T(8,128)(2,1)}, u32[]{:S(2)}, u32[]{:S(2)}) async-start(bf16[128,3,3,16,128]{4,3,2,1,0:T(8,128)(2,1)} %bitcast.51), calls=%async_computation.1 | async-start | bytes 9437184 | tf_op jit(solution)/shard_map/all_to_all | solution.py:252
  235.1 0.0 copy-start.5
  235.1 0.0 copy-start.7
  235.1 1.1 broadcast_in_dim.28
  236.3 0.0 copy-start.9
  236.3 0.2 bitcast_dynamic-update-slice_fusion
  236.5 0.0 copy-start.3
  236.5 1.3 bitcast_dynamic-update-slice_fusion.7
  237.8 0.0 copy-done.5
  237.8 0.1 bitcast_dynamic-update-slice_fusion.6
  237.9 0.0 copy-done.7
  237.9 0.1 bitcast_dynamic-update-slice_fusion.5
  238.0 1.1 bitcast_dynamic-update-slice_fusion.4
  239.1 1.1 bitcast_dynamic-update-slice_fusion.3
  240.3 1.1 bitcast_dynamic-update-slice_fusion.2
  241.4 0.1 bitcast_dynamic-update-slice_fusion.1
  241.5 8.0 %gate.1.g_ref = bf16[48,384,128]{2,1,0:T(8,128)(2,1)S(1)} custom-call(bf16[48,384,128]{2,1,0:T(8,128)(2,1)S(1)} %bitcast.45, bf16[128,128]{1,0:T(8,128)(2,1)S(1)} %copy-done.3), custom_call_target="tpu_custom_call" | custom-call | flops 603979776 | bytes 14155776 | tf_op jit(solution)/shard_map/gate/pallas_call | solution.py:130
  249.6 2.2 copy-done
  251.8 2.2 copy-done.2
  254.0 39.3 %all-to-all-done.1.r_ref = bf16[128,3,3,16,128]{4,3,2,1,0:T(8,128)(2,1)} async-done(((bf16[128,3,3,16,128]{4,3,2,1,0:T(8,128)(2,1)}), bf16[128,3,3,16,128]{4,3,2,1,0:T(8,128)(2,1)}, u32[]{:S(2)}, u32[]{:S(2)}) %all-to-all-start.1) | async-done | bytes 4718624 | tf_op jit(solution)/shard_map/all_to_all | solution.py:252
  293.3 10.7 %finish.1 = bf16[48,384,128]{2,1,0:T(8,128)(2,1)} custom-call(bf16[128,3,3,16,128]{4,3,2,1,0:T(8,128)(2,1)} %all-to-all-done.1.r_ref, bf16[48,384,128]{2,1,0:T(8,128)(2,1)} %bitcast.46, bf16[48,384,128]{2,1,0:T(8,128)(2,1)} %copy-done.2, bf16[128,128]{1,0:T(8,128)(2,1)} %w_ref.3), custom_call_target="tpu_custom_call" | custom-call | flops 603979776 | bytes 18874368 | tf_op jit(solution)/shard_map/finish/pallas_call | solution.py:178
  (7 shorter events, 0.0 us)
Async XLA Ops:
  3.4 31.9 %collective-permute-start.2 = (bf16[48,48,128]{2,0,1:T(8,128)(2,1)S(1)}, bf16[48,48,128]{2,0,1:T(8,128)(2,1)S(1)}, u32[]{:S(2)}, u32[]{:S(2)}) collective-permute-start(bf16[48,48,128]{2,0,1:T(8,128)(2,1)S(1)} %bitcast.52), channel_id=1, source_target_pairs={{2,66},{3,98},{6,70},{7,102},{10,74},{11,106},{14,78},{15,110},{18... | collective-permute-start | bytes 1769480 | tf_op jit(solution)/shard_map/ppermute | solution.py:218
  5.6 29.7 %collective-permute-start.3 = (bf16[48,48,128]{2,0,1:T(8,128)(2,1)}, bf16[48,48,128]{2,0,1:T(8,128)(2,1)S(1)}, u32[]{:S(2)}, u32[]{:S(2)}) collective-permute-start(bf16[48,48,128]{2,0,1:T(8,128)(2,1)} %bitcast.41), channel_id=1, source_target_pairs={{2,70},{3,102},{6,66},{7,98},{10,78},{11,110},{14,74},{15,106},{18... | collective-permute-start | bytes 1769480 | tf_op jit(solution)/shard_map/ppermute | solution.py:218
  6.9 45.6 %collective-permute-start.8 = (bf16[48,48,128]{2,0,1:T(8,128)(2,1)S(1)}, bf16[48,48,128]{2,0,1:T(8,128)(2,1)S(1)}, u32[]{:S(2)}, u32[]{:S(2)}) collective-permute-start(bf16[48,48,128]{2,0,1:T(8,128)(2,1)S(1)} %bitcast.53), channel_id=1, source_target_pairs={{0,0},{1,32},{4,4},{5,36},{8,8},{9,40},{12,12},{13,44},{16,16},{17... | collective-permute-start | bytes 1769480 | tf_op jit(solution)/shard_map/ppermute | solution.py:218
  11.5 42.9 %copy-start.11 = (bf16[128,512]{1,0:T(8,128)(2,1)S(1)}, bf16[128,512]{1,0:T(8,128)(2,1)}, u32[]{:S(2)}) copy-start(bf16[128,512]{1,0:T(8,128)(2,1)} %param.5) | copy-start | bytes 393220
  11.7 32.1 %collective-permute-start = (bf16[48,48,128]{2,0,1:T(8,128)(2,1)S(1)}, bf16[48,48,128]{2,0,1:T(8,128)(2,1)S(1)}, u32[]{:S(2)}, u32[]{:S(2)}) collective-permute-start(bf16[48,48,128]{2,0,1:T(8,128)(2,1)S(1)} %bitcast.55), channel_id=1, source_target_pairs={{0,8},{1,40},{2,72},{3,104},{4,12},{5,44},{6,76},{7,108},{8,0},{9,... | collective-permute-start | bytes 1769480 | tf_op jit(solution)/shard_map/ppermute | solution.py:218
  13.3 35.6 %collective-permute-start.1 = (bf16[48,48,128]{2,0,1:T(8,128)(2,1)S(1)}, bf16[48,48,128]{2,0,1:T(8,128)(2,1)S(1)}, u32[]{:S(2)}, u32[]{:S(2)}) collective-permute-start(bf16[48,48,128]{2,0,1:T(8,128)(2,1)S(1)} %bitcast.54), channel_id=1, source_target_pairs={{0,12},{1,44},{2,76},{3,108},{4,8},{5,40},{6,72},{7,104},{8,4},{9,... | collective-permute-start | bytes 1769480 | tf_op jit(solution)/shard_map/ppermute | solution.py:218
  35.4 56.9 %collective-permute-start.7 = (bf16[96,48,128]{2,0,1:T(8,128)(2,1)S(1)}, bf16[96,48,128]{2,0,1:T(8,128)(2,1)S(1)}, u32[]{:S(2)}, u32[]{:S(2)}) collective-permute-start(bf16[96,48,128]{2,0,1:T(8,128)(2,1)S(1)} %pad_maximum_fusion), channel_id=1, source_target_pairs={{0,2},{1,3},{4,6},{5,7},{8,10},{9,11},{12,14},{13,15},{16,18},{17,... | collective-permute-start | bytes 3538952 | tf_op jit(solution)/shard_map/ppermute | solution.py:218
  39.7 30.0 %collective-permute-start.4 = (bf16[48,48,128]{2,0,1:T(8,128)(2,1)}, bf16[48,48,128]{2,0,1:T(8,128)(2,1)}, u32[]{:S(2)}, u32[]{:S(2)}) collective-permute-start(bf16[48,48,128]{2,0,1:T(8,128)(2,1)} %get-tuple-element.26), channel_id=1, source_target_pairs={{0,16},{1,48},{2,80},{3,112},{4,20},{5,52},{6,84},{7,116},{8,24},{... | collective-permute-start | bytes 1769480 | tf_op jit(solution)/shard_map/ppermute | solution.py:218
  43.8 8.7 %copy-start.4 = (bf16[48,48,128]{2,0,1:T(8,128)(2,1)}, bf16[48,48,128]{2,0,1:T(8,128)(2,1)S(1)}, u32[]{:S(2)}) copy-start(bf16[48,48,128]{2,0,1:T(8,128)(2,1)S(1)} %collective-permute-done) | copy-start | bytes 1769476
  43.8 40.2 %collective-permute-start.5 = (bf16[48,48,128]{2,0,1:T(8,128)(2,1)}, bf16[48,48,128]{2,0,1:T(8,128)(2,1)}, u32[]{:S(2)}, u32[]{:S(2)}) collective-permute-start(bf16[48,48,128]{2,0,1:T(8,128)(2,1)} %get-tuple-element.27), channel_id=1, source_target_pairs={{0,20},{1,52},{2,84},{3,116},{4,16},{5,48},{6,80},{7,112},{8,28},{... | collective-permute-start | bytes 1769480 | tf_op jit(solution)/shard_map/ppermute | solution.py:218
  48.9 3.6 %copy-start.6 = (bf16[48,48,128]{2,0,1:T(8,128)(2,1)}, bf16[48,48,128]{2,0,1:T(8,128)(2,1)S(1)}, u32[]{:S(2)}) copy-start(bf16[48,48,128]{2,0,1:T(8,128)(2,1)S(1)} %collective-permute-done.1) | copy-start | bytes 1769476
  48.9 35.1 %collective-permute-start.6 = (bf16[48,48,128]{2,0,1:T(8,128)(2,1)}, bf16[48,48,128]{2,0,1:T(8,128)(2,1)}, u32[]{:S(2)}, u32[]{:S(2)}) collective-permute-start(bf16[48,48,128]{2,0,1:T(8,128)(2,1)} %get-tuple-element.28), channel_id=1, source_target_pairs={{0,24},{1,56},{2,88},{3,120},{4,28},{5,60},{6,92},{7,124},{8,16},{... | collective-permute-start | bytes 1769480 | tf_op jit(solution)/shard_map/ppermute | solution.py:218
  52.5 39.8 %collective-permute-start.9 = (bf16[48,48,128]{2,0,1:T(8,128)(2,1)}, bf16[48,48,128]{2,0,1:T(8,128)(2,1)}, u32[]{:S(2)}, u32[]{:S(2)}) collective-permute-start(bf16[48,48,128]{2,0,1:T(8,128)(2,1)} %bitcast.41), channel_id=1, source_target_pairs={{0,4},{1,36},{4,0},{5,32},{8,12},{9,44},{12,8},{13,40},{16,20},{17... | collective-permute-start | bytes 1769480 | tf_op jit(solution)/shard_map/ppermute | solution.py:218
  54.6 2.3 copy-start.1
  69.8 139.0 %copy-start.10 = (bf16[48,48,128]{2,0,1:T(8,128)(2,1)S(1)}, bf16[48,48,128]{2,0,1:T(8,128)(2,1)}, u32[]{:S(2)}) copy-start(bf16[48,48,128]{2,0,1:T(8,128)(2,1)} %get-tuple-element.35) | copy-start | bytes 1769476
  208.8 18.5 %collective-permute-start.10 = (bf16[48,48,128]{2,0,1:T(8,128)(2,1)S(1)}, bf16[48,48,128]{2,0,1:T(8,128)(2,1)S(1)}, u32[]{:S(2)}, u32[]{:S(2)}) collective-permute-start(bf16[48,48,128]{2,0,1:T(8,128)(2,1)S(1)} %copy-done.10), channel_id=1, source_target_pairs={{0,28},{1,60},{2,92},{3,124},{4,24},{5,56},{6,88},{7,120},{8,20},{... | collective-permute-start | bytes 1769480 | tf_op jit(solution)/shard_map/ppermute | solution.py:218
  227.3 0.9 copy-start.8
  228.1 65.2 %all-to-all-start.1 = ((bf16[128,3,3,16,128]{4,3,2,1,0:T(8,128)(2,1)}), bf16[128,3,3,16,128]{4,3,2,1,0:T(8,128)(2,1)}, u32[]{:S(2)}, u32[]{:S(2)}) async-start(bf16[128,3,3,16,128]{4,3,2,1,0:T(8,128)(2,1)} %bitcast.51), calls=%async_computation.1 | async-start | bytes 9437184 | tf_op jit(solution)/shard_map/all_to_all | solution.py:252
  235.1 2.7 copy-start.5
  235.1 2.7 copy-start.7
  236.3 5.2 %copy-start.9 = (bf16[48,48,128]{2,0,1:T(8,128)(2,1)S(1)}, bf16[48,48,128]{2,0,1:T(8,128)(2,1)}, u32[]{:S(2)}) copy-start(bf16[48,48,128]{2,0,1:T(8,128)(2,1)} %copy-done.8) | copy-start | bytes 1769476
  236.5 5.0 %copy-start.3 = (bf16[128,128]{1,0:T(8,128)(2,1)S(1)}, bf16[128,128]{1,0:T(8,128)(2,1)}, u32[]{:S(2)}) copy-start(bf16[128,128]{1,0:T(8,128)(2,1)} %w_ref.2) | copy-start | bytes 98308
  249.6 2.2 copy-start
  251.8 2.2 copy-start.2
